TPU v7x, 256 devices: a whole 4x4x8 slice. The times are simulated.
256 devices in a mesh: seq: 64 (over y_lo, z, x), chan: 4 (over y_hi, core).
Axes of the slice: x: 4, y: 4 (y_hi: 2, y_lo: 2; y = y_hi * 2 + y_lo), z: 8, core: 2. Of those that a mesh axis runs over, the one named last changes fastest.
Arguments:
- out_gate: bfloat16 [32768, 2048], P('seq', 'chan'), may hold values from -6 to 6
- in_gate: bfloat16 [32768, 2048], P('seq', 'chan'), may hold values from -6 to 6
- values: bfloat16 [32768, 2048], P('seq', 'chan'), may hold values from -6 to 6
- filter_param: bfloat16 [32768, 2048], P('seq', 'chan'), may hold values from -193.49419 to 193.49419
- out_weight: bfloat16 [2048, 2048], P('chan'), may hold values from -0.125 to 0.125
- out_cotangent: bfloat16 [32768, 2048], P(('seq', 'chan')), may hold values from -6 to 6
Outputs:
- output: bfloat16 [32768, 2048], P(('seq', 'chan'))
- d_out_gate: float32 [32768, 2048], P('seq', 'chan')
- d_in_gate: float32 [32768, 2048], P('seq', 'chan')
- d_values: float32 [32768, 2048], P('seq', 'chan')
- d_filter: float32 [32768, 2048], P('seq', 'chan')
All inputs are finite; a program needn't handle non-finite values.
Results may differ from a plain program's by a relative error of at most 0.006.
Values may be sent and summed in bfloat16 or wider, within the bound.
A program may use at most 128 MiB of HBM per device.

v0:
```python
import math

import jax
import jax.numpy as jnp
from jax import lax
from jax.sharding import PartitionSpec as P

HIGHEST_PREC = lax.Precision.HIGHEST
TWO_PI = 2.0 * math.pi


def phase_pair(numer, denom, sign):
    angles = sign * TWO_PI / denom * (numer % denom).astype(jnp.float32)
    return (jnp.cos(angles), jnp.sin(angles))


def complex_dot(table, operand, form):
    real_part = jnp.einsum(form, table[0], operand[0], precision=HIGHEST_PREC) - jnp.einsum(
        form, table[1], operand[1], precision=HIGHEST_PREC
    )
    imag_part = jnp.einsum(form, table[0], operand[1], precision=HIGHEST_PREC) + jnp.einsum(
        form, table[1], operand[0], precision=HIGHEST_PREC
    )
    return (real_part, imag_part)


def complex_mul(left, right):
    return (left[0] * right[0] - left[1] * right[1], left[0] * right[1] + left[1] * right[0])


def conjugate(pair_value):
    return (pair_value[0], -pair_value[1])


def slot_order(parts):
    slots = jnp.arange(parts, dtype=jnp.int32)
    paired = jnp.where(slots % 2 == 0, slots // 2, parts - (slots - 1) // 2)
    return jnp.where(slots == 0, 0, jnp.where(slots == 1, parts // 2, paired))


def pair_rows(piece):
    parts = piece.shape[0]
    flipped = piece.reshape((parts // 2, 2) + piece.shape[1:])[:, ::-1].reshape(piece.shape)
    return jnp.concatenate([piece[:2], flipped[2:]], 0)


def pack_pair(spectrum, half_cols):
    first_re, first_im = (spectrum[0][:, :half_cols], spectrum[1][:, :half_cols])
    second_re, second_im = (spectrum[0][:, half_cols:], spectrum[1][:, half_cols:])
    return (first_re - second_im, first_im + second_re)


def forward_spectra(real_in, imag_in, square_table):
    parts = lax.axis_size("seq")
    my_index = lax.axis_index("seq")
    tok_rows = real_in.shape[0]
    total = tok_rows * parts
    block_rows = tok_rows // parts
    order = slot_order(parts)
    across_table = phase_pair(
        order[:, None] * jnp.arange(parts, dtype=jnp.int32)[None, :], parts, -1.0
    )
    global_rows = my_index * block_rows + jnp.arange(block_rows, dtype=jnp.int32)
    twist = phase_pair(order[:, None] * global_rows[None, :], total, -1.0)
    stacked_in = jnp.stack([real_in, imag_in])[:, None]
    pieces = lax.all_to_all(stacked_in, "seq", split_axis=2, concat_axis=1, tiled=True)
    mixed = complex_dot(across_table, (pieces[0], pieces[1]), "pa,abc->pbc")
    turned = complex_mul(mixed, (twist[0][:, :, None], twist[1][:, :, None]))
    moved = jnp.stack([turned[0], turned[1]])
    columns = (moved[0], moved[1])
    stacked = (
        jnp.stack([columns[0], pair_rows(columns[0])], 1),
        jnp.stack([columns[1], pair_rows(columns[1])], 1),
    )
    arrived = (
        lax.all_to_all(stacked[0], "seq", split_axis=0, concat_axis=2, tiled=True),
        lax.all_to_all(stacked[1], "seq", split_axis=0, concat_axis=2, tiled=True),
    )
    both = complex_dot(square_table, (arrived[0][0], arrived[1][0]), "kb,sbc->skc")
    own = (both[0][0], both[1][0])
    source = (both[0][1], both[1][1])
    mirrored = tuple(
        (
            jnp.where(my_index == 0, jnp.roll(flipped, 1, axis=0), flipped)
            for flipped in (source[0][::-1], source[1][::-1])
        )
    )
    first = (0.5 * (own[0] + mirrored[0]), 0.5 * (own[1] - mirrored[1]))
    second = (0.5 * (own[1] + mirrored[1]), 0.5 * (mirrored[0] - own[0]))
    return (first, second)


def inverse_tokens(spectrum, square_table):
    parts = lax.axis_size("seq")
    my_index = lax.axis_index("seq")
    tok_rows = spectrum[0].shape[0]
    total = tok_rows * parts
    order = slot_order(parts)
    back_table = (square_table[0], -square_table[1])
    local_rows = complex_dot(back_table, spectrum, "bk,kc->bc")
    twist = phase_pair(order[my_index] * jnp.arange(tok_rows, dtype=jnp.int32), total, 1.0)
    weighted = complex_mul(local_rows, (twist[0][:, None] / total, twist[1][:, None] / total))
    across_table = phase_pair(
        jnp.arange(parts, dtype=jnp.int32)[:, None] * order[None, :], parts, 1.0
    )
    stacked_in = jnp.stack([weighted[0], weighted[1]])[:, None]
    pieces = lax.all_to_all(stacked_in, "seq", split_axis=2, concat_axis=1, tiled=True)
    mixed_pair = complex_dot(across_table, (pieces[0], pieces[1]), "pa,abc->pbc")
    mixed = jnp.stack([mixed_pair[0], mixed_pair[1]])
    landed = (
        lax.all_to_all(mixed[0], "seq", split_axis=0, concat_axis=1, tiled=True),
        lax.all_to_all(mixed[1], "seq", split_axis=0, concat_axis=1, tiled=True),
    )
    return (landed[0][0], landed[1][0])


def on_device(out_gate, in_gate, values, filter_param, out_weight, out_cotangent):
    tok_rows, width_cols = values.shape
    half_cols = width_cols // 2
    total = tok_rows * lax.axis_size("seq")
    scale_factor = 1.0 / math.sqrt(total)
    gate_after = out_gate.astype(jnp.float32)
    position_numbers = jnp.arange(tok_rows, dtype=jnp.int32)
    square_table = phase_pair(position_numbers[:, None] * position_numbers[None, :], tok_rows, -1.0)
    gate_before = in_gate.astype(jnp.float32)
    value_cols = values.astype(jnp.float32)
    source = gate_before * value_cols
    kernel = filter_param.astype(jnp.float32) * scale_factor
    first, second = forward_spectra(
        jnp.concatenate([source[:, :half_cols], kernel[:, :half_cols]], 1),
        jnp.concatenate([source[:, half_cols:], kernel[:, half_cols:]], 1),
        square_table,
    )
    source_spec = tuple(
        (
            jnp.concatenate([first[part_id][:, :half_cols], second[part_id][:, :half_cols]], 1)
            for part_id in range(2)
        )
    )
    kernel_spec = tuple(
        (
            jnp.concatenate([first[part_id][:, half_cols:], second[part_id][:, half_cols:]], 1)
            for part_id in range(2)
        )
    )
    conv_re, conv_im = inverse_tokens(
        pack_pair(complex_mul(source_spec, kernel_spec), half_cols), square_table
    )
    conv = jnp.concatenate([conv_re, conv_im], 1)
    gated = (gate_after * conv).astype(jnp.bfloat16)
    output = lax.psum_scatter(
        jnp.dot(gated, out_weight, preferred_element_type=jnp.float32),
        "chan",
        scatter_dimension=0,
        tiled=True,
    ).astype(jnp.bfloat16)
    d_gated = lax.dot_general(
        lax.all_gather(out_cotangent, "chan", axis=0, tiled=True),
        out_weight,
        (((1,), (1,)), ((), ())),
        preferred_element_type=jnp.float32,
    )
    d_after = d_gated * conv
    d_conv = d_gated * gate_after
    first, second = forward_spectra(d_conv[:, :half_cols], d_conv[:, half_cols:], square_table)
    conv_spec = tuple(
        (jnp.concatenate([first[part_id], second[part_id]], 1) for part_id in range(2))
    )
    packed_source = pack_pair(complex_mul(conjugate(kernel_spec), conv_spec), half_cols)
    packed_kernel = pack_pair(complex_mul(conjugate(source_spec), conv_spec), half_cols)
    joined = (
        jnp.concatenate([packed_source[0], packed_kernel[0]], 1),
        jnp.concatenate([packed_source[1], packed_kernel[1]], 1),
    )
    real_out, imag_out = inverse_tokens(joined, square_table)
    d_source = jnp.concatenate([real_out[:, :half_cols], imag_out[:, :half_cols]], 1)
    d_kernel = jnp.concatenate([real_out[:, half_cols:], imag_out[:, half_cols:]], 1)
    d_before = d_source * value_cols
    d_value = d_source * gate_before
    d_filter = d_kernel * scale_factor
    return (output, d_after, d_before, d_value, d_filter)


def solution(mesh):
    return jax.shard_map(
        on_device,
        mesh=mesh,
        in_specs=(
            P("seq", "chan"),
            P("seq", "chan"),
            P("seq", "chan"),
            P("seq", "chan"),
            P("chan", None),
            P(("seq", "chan"), None),
        ),
        out_specs=(
            P(("seq", "chan"), None),
            P("seq", "chan"),
            P("seq", "chan"),
            P("seq", "chan"),
            P("seq", "chan"),
        ),
        check_vma=False,
    )
```

profile of v0, /device:TPU:1, one launch (start us, length us, event | category | flops | bytes accessed | tf_op | source)
XLA Modules:
  0.0 702.0 jit_solution(13447763220499388029)
XLA Ops:
  13.0 13.9 %all-to-all-start = ((f32[2,1,512,512]{3,1,0,2:T(1,128)}), f32[2,1,512,512]{3,1,0,2:T(1,128)}, u32[]{:S(2)}, u32[]{:S(2)}) async-start(f32[2,1,512,512]{3,1,0,2:T(1,128)} %copy.105), calls=%async_computation | async-start | bytes 4194304 | tf_op jit(solution)/shard_map/all_to_all | solution.py:66
  27.1 47.2 %all-to-all-done = f32[2,1,512,512]{3,1,0,2:T(1,128)} async-done(((f32[2,1,512,512]{3,1,0,2:T(1,128)}), f32[2,1,512,512]{3,1,0,2:T(1,128)}, u32[]{:S(2)}, u32[]{:S(2)}) %all-to-all-start) | async-done | bytes 2097184 | tf_op jit(solution)/shard_map/all_to_all | solution.py:66
  93.7 9.8 %all-to-all-start.1 = ((f32[64,2,8,512]{3,2,1,0:T(8,128)}), f32[64,2,8,512]{3,2,1,0:T(8,128)}, u32[]{:S(2)}, u32[]{:S(2)}) async-start(f32[64,2,8,512]{3,2,1,0:T(8,128)} %copy.114), calls=%async_computation.1 | async-start | bytes 4194304 | tf_op jit(solution)/shard_map/all_to_all | solution.py:76
  112.2 38.2 %all-to-all-done.1 = f32[64,2,8,512]{3,2,1,0:T(8,128)} async-done(((f32[64,2,8,512]{3,2,1,0:T(8,128)}), f32[64,2,8,512]{3,2,1,0:T(8,128)}, u32[]{:S(2)}, u32[]{:S(2)}) %all-to-all-start.1) | async-done | bytes 2097184 | tf_op jit(solution)/shard_map/all_to_all | solution.py:76
  150.4 8.9 %all-to-all-start.2 = ((f32[64,2,8,512]{3,2,1,0:T(8,128)}), f32[64,2,8,512]{3,2,1,0:T(8,128)}, u32[]{:S(2)}, u32[]{:S(2)}) async-start(f32[64,2,8,512]{3,2,1,0:T(8,128)} %copy.118), calls=%async_computation.2 | async-start | bytes 4194304 | tf_op jit(solution)/shard_map/all_to_all | solution.py:77
  160.7 10.3 %fusion.2 = f32[2,512,512]{1,2,0:T(8,128)} fusion(f32[64,2,8,512]{3,2,1,0:T(8,128)} %all-to-all-done.1), kind=kOutput, calls=%fused_computation.6 | convolution fusion | flops 3224895488 | bytes 4194304 | tf_op jit(solution)/shard_map/kb,sbc->skc/dot_general | solution.py:18
  171.0 35.0 %all-to-all-done.2 = f32[64,2,8,512]{3,2,1,0:T(8,128)} async-done(((f32[64,2,8,512]{3,2,1,0:T(8,128)}), f32[64,2,8,512]{3,2,1,0:T(8,128)}, u32[]{:S(2)}, u32[]{:S(2)}) %all-to-all-start.2) | async-done | bytes 2097184 | tf_op jit(solution)/shard_map/all_to_all | solution.py:77
  206.0 9.8 %subtract_bitcast_fusion = f32[2,512,512]{2,1,0:T(8,128)S(1)} fusion(f32[2,512,512]{1,2,0:T(8,128)} %fusion.2, f32[64,2,8,512]{3,2,1,0:T(8,128)} %all-to-all-done.2), kind=kOutput, calls=%fused_computation.13 | convolution fusion | flops 3225419776 | bytes 6291456 | tf_op jit(solution)/shard_map/kb,sbc->skc/dot_general | solution.py:18
  218.1 8.9 %fusion = f32[2,512,512]{1,2,0:T(8,128)S(1)} fusion(f32[64,2,8,512]{3,2,1,0:T(8,128)} %all-to-all-done.1), kind=kOutput, calls=%fused_computation.4 | convolution fusion | flops 3224895488 | bytes 4194304 | tf_op jit(solution)/shard_map/kb,sbc->skc/dot_general | solution.py:21
  227.0 9.4 %add_bitcast_fusion = f32[2,512,512]{2,1,0:T(8,128)S(1)} fusion(f32[2,512,512]{1,2,0:T(8,128)S(1)} %fusion, f32[64,2,8,512]{3,2,1,0:T(8,128)} %all-to-all-done.2), kind=kOutput, calls=%fused_computation.12 | convolution fusion | flops 3225419776 | bytes 6291456 | tf_op jit(solution)/shard_map/kb,sbc->skc/dot_general | solution.py:21
  246.0 9.1 %slice.307 = f32[511,512]{1,0:T(8,128)} reverse(f32[511,512]{1,0:T(8,128)} %slice_bitcast_fusion.4), dimensions={0} | reverse | bytes 2093056 | tf_op jit(solution)/shard_map/jit(_roll_static)/slice | solution.py:84
  258.1 9.0 %rev.17 = f32[512,512]{1,0:T(8,128)} reverse(f32[512,512]{1,0:T(8,128)} %slice_bitcast_fusion), dimensions={0} | reverse | bytes 2097152 | tf_op jit(solution)/shard_map/rev | solution.py:85
  267.1 9.1 %slice.315 = f32[511,512]{1,0:T(8,128)} reverse(f32[511,512]{1,0:T(8,128)} %slice_bitcast_fusion.1), dimensions={0} | reverse | bytes 2093056 | tf_op jit(solution)/shard_map/jit(_roll_static)/slice | solution.py:84
  302.5 8.6 %all-to-all-start.3 = ((f32[2,1,512,256]{3,0,1,2:T(2,128)}), f32[2,1,512,256]{3,0,1,2:T(2,128)S(1)}, u32[]{:S(2)}, u32[]{:S(2)}) async-start(f32[2,1,512,256]{3,0,1,2:T(2,128)} %copy.120), calls=%async_computation.3 | async-start | bytes 2097152 | tf_op jit(solution)/shard_map/all_to_all | solution.py:107
  311.9 24.2 %all-to-all-done.3 = f32[2,1,512,256]{3,0,1,2:T(2,128)S(1)} async-done(((f32[2,1,512,256]{3,0,1,2:T(2,128)}), f32[2,1,512,256]{3,0,1,2:T(2,128)S(1)}, u32[]{:S(2)}, u32[]{:S(2)}) %all-to-all-start.3) | async-done | bytes 1048608 | tf_op jit(solution)/shard_map/all_to_all | solution.py:107
  350.3 10.9 %all-to-all-done.4 = f32[64,8,256]{2,1,0:T(8,128)} async-done(((f32[64,8,256]{2,1,0:T(8,128)}), f32[64,8,256]{2,1,0:T(8,128)}, u32[]{:S(2)}, u32[]{:S(2)}) %all-to-all-start.4) | async-done | bytes 524320 | tf_op jit(solution)/shard_map/all_to_all | solution.py:111
  368.6 13.8 %all-to-all-done.5 = f32[64,8,256]{2,1,0:T(8,128)S(1)} async-done(((f32[64,8,256]{2,1,0:T(8,128)}), f32[64,8,256]{2,1,0:T(8,128)S(1)}, u32[]{:S(2)}, u32[]{:S(2)}) %all-to-all-start.5) | async-done | bytes 524320 | tf_op jit(solution)/shard_map/all_to_all | solution.py:112
  387.5 30.6 %all_to_all.132 = f32[2,1,512,256]{3,0,1,2:T(2,128)S(1)} all-to-all(f32[2,1,512,256]{3,0,1,2:T(2,128)S(1)} %copy.129), channel_id=1, replica_groups=mesh['seq'=64,'chan'=4] {'seq'}, dimensions={2} | all-to-all | bytes 2097152 | tf_op jit(solution)/shard_map/all_to_all | solution.py:66
  441.1 18.9 %all-to-all-done.8 = f32[64,2,8,256]{3,2,1,0:T(8,128)} async-done(((f32[64,2,8,256]{3,2,1,0:T(8,128)}), f32[64,2,8,256]{3,2,1,0:T(8,128)}, u32[]{:S(2)}, u32[]{:S(2)}) %all-to-all-start.8) | async-done | bytes 1048608 | tf_op jit(solution)/shard_map/all_to_all | solution.py:77
  475.9 15.2 %all-to-all-done.7 = f32[64,2,8,256]{3,2,1,0:T(8,128)S(1)} async-done(((f32[64,2,8,256]{3,2,1,0:T(8,128)}), f32[64,2,8,256]{3,2,1,0:T(8,128)S(1)}, u32[]{:S(2)}, u32[]{:S(2)}) %all-to-all-start.7) | async-done | bytes 1048608 | tf_op jit(solution)/shard_map/all_to_all | solution.py:76
  578.4 39.2 %all-to-all-done.9 = f32[2,1,512,512]{3,0,1,2:T(2,128)} async-done(((f32[2,1,512,512]{3,0,1,2:T(2,128)}), f32[2,1,512,512]{3,0,1,2:T(2,128)}, u32[]{:S(2)}, u32[]{:S(2)}) %all-to-all-start.9) | async-done | bytes 2097184 | tf_op jit(solution)/shard_map/all_to_all | solution.py:107
  626.7 10.3 %all-to-all-start.10 = ((f32[64,8,512]{2,1,0:T(8,128)}), f32[64,8,512]{2,1,0:T(8,128)}, u32[]{:S(2)}, u32[]{:S(2)}) async-start(f32[64,8,512]{2,1,0:T(8,128)} %copy.157), calls=%async_computation.11 | async-start | bytes 2097152 | tf_op jit(solution)/shard_map/all_to_all | solution.py:111
  643.2 16.9 %all-to-all-done.10 = f32[64,8,512]{2,1,0:T(8,128)} async-done(((f32[64,8,512]{2,1,0:T(8,128)}), f32[64,8,512]{2,1,0:T(8,128)}, u32[]{:S(2)}, u32[]{:S(2)}) %all-to-all-start.10) | async-done | bytes 1048608 | tf_op jit(solution)/shard_map/all_to_all | solution.py:111
  672.3 18.8 %all-to-all-done.11 = f32[64,8,512]{2,1,0:T(8,128)S(1)} async-done(((f32[64,8,512]{2,1,0:T(8,128)}), f32[64,8,512]{2,1,0:T(8,128)S(1)}, u32[]{:S(2)}, u32[]{:S(2)}) %all-to-all-start.11) | async-done | bytes 1048608 | tf_op jit(solution)/shard_map/all_to_all | solution.py:112
  (214 shorter events, 260.4 us)
Async XLA Ops:
  7.2 375.3 %copy-start = (bf16[512,2048]{1,0:T(8,128)(2,1)S(1)}, bf16[512,2048]{1,0:T(8,128)(2,1)}, u32[]{:S(2)}) copy-start(bf16[512,2048]{1,0:T(8,128)(2,1)} %param.10) | copy-start | bytes 6291460
  13.0 61.3 %all-to-all-start = ((f32[2,1,512,512]{3,1,0,2:T(1,128)}), f32[2,1,512,512]{3,1,0,2:T(1,128)}, u32[]{:S(2)}, u32[]{:S(2)}) async-start(f32[2,1,512,512]{3,1,0,2:T(1,128)} %copy.105), calls=%async_computation | async-start | bytes 4194304 | tf_op jit(solution)/shard_map/all_to_all | solution.py:66
  93.7 56.8 %all-to-all-start.1 = ((f32[64,2,8,512]{3,2,1,0:T(8,128)}), f32[64,2,8,512]{3,2,1,0:T(8,128)}, u32[]{:S(2)}, u32[]{:S(2)}) async-start(f32[64,2,8,512]{3,2,1,0:T(8,128)} %copy.114), calls=%async_computation.1 | async-start | bytes 4194304 | tf_op jit(solution)/shard_map/all_to_all | solution.py:76
  150.4 55.6 %all-to-all-start.2 = ((f32[64,2,8,512]{3,2,1,0:T(8,128)}), f32[64,2,8,512]{3,2,1,0:T(8,128)}, u32[]{:S(2)}, u32[]{:S(2)}) async-start(f32[64,2,8,512]{3,2,1,0:T(8,128)} %copy.118), calls=%async_computation.2 | async-start | bytes 4194304 | tf_op jit(solution)/shard_map/all_to_all | solution.py:77
  258.1 21.8 %copy-start.6 = (f32[512,256]{1,0:T(8,128)}, f32[512,256]{1,0:T(8,128)S(1)}, u32[]{:S(2)}) copy-start(f32[512,256]{1,0:T(8,128)S(1)} %get-tuple-element.50) | copy-start | bytes 1572868
  258.1 21.8 %copy-start.8 = (f32[512,256]{1,0:T(8,128)}, f32[512,256]{1,0:T(8,128)S(1)}, u32[]{:S(2)}) copy-start(f32[512,256]{1,0:T(8,128)S(1)} %get-tuple-element.49) | copy-start | bytes 1572868
  302.5 33.5 %all-to-all-start.3 = ((f32[2,1,512,256]{3,0,1,2:T(2,128)}), f32[2,1,512,256]{3,0,1,2:T(2,128)S(1)}, u32[]{:S(2)}, u32[]{:S(2)}) async-start(f32[2,1,512,256]{3,0,1,2:T(2,128)} %copy.120), calls=%async_computation.3 | async-start | bytes 2097152 | tf_op jit(solution)/shard_map/all_to_all | solution.py:107
  311.1 57.5 %all-gather.2.cloned.1.call-start = ((), (), s32[]{:S(2)}) async-start(), calls=%async_computation.14 | async-start | bytes 2621440 | tf_op jit(solution)/shard_map/all_gather | solution.py:158
  339.6 21.6 %all-to-all-start.4 = ((f32[64,8,256]{2,1,0:T(8,128)}), f32[64,8,256]{2,1,0:T(8,128)}, u32[]{:S(2)}, u32[]{:S(2)}) async-start(f32[64,8,256]{2,1,0:T(8,128)} %copy.125), calls=%async_computation.4 | async-start | bytes 1048576 | tf_op jit(solution)/shard_map/all_to_all | solution.py:111
  348.4 34.0 %copy-start.33 = (bf16[512,512]{1,0:T(8,128)(2,1)S(1)}, bf16[512,512]{1,0:T(8,128)(2,1)}, u32[]{:S(2)}) copy-start(bf16[512,512]{1,0:T(8,128)(2,1)} %param.6) | copy-start | bytes 1572868
  361.2 21.2 %all-to-all-start.5 = ((f32[64,8,256]{2,1,0:T(8,128)}), f32[64,8,256]{2,1,0:T(8,128)S(1)}, u32[]{:S(2)}, u32[]{:S(2)}) async-start(f32[64,8,256]{2,1,0:T(8,128)} %copy.128), calls=%async_computation.5 | async-start | bytes 1048576 | tf_op jit(solution)/shard_map/all_to_all | solution.py:112
  382.4 4.1 copy-start.31
  428.7 31.2 %all-to-all-start.8 = ((f32[64,2,8,256]{3,2,1,0:T(8,128)}), f32[64,2,8,256]{3,2,1,0:T(8,128)}, u32[]{:S(2)}, u32[]{:S(2)}) async-start(f32[64,2,8,256]{3,2,1,0:T(8,128)} %copy.143), calls=%async_computation.9 | async-start | bytes 2097152 | tf_op jit(solution)/shard_map/all_to_all | solution.py:77
  459.9 31.3 %all-to-all-start.7 = ((f32[64,2,8,256]{3,2,1,0:T(8,128)}), f32[64,2,8,256]{3,2,1,0:T(8,128)S(1)}, u32[]{:S(2)}, u32[]{:S(2)}) async-start(f32[64,2,8,256]{3,2,1,0:T(8,128)} %copy.138), calls=%async_computation.8 | async-start | bytes 2097152 | tf_op jit(solution)/shard_map/all_to_all | solution.py:76
  498.1 7.6 %copy-start.23 = (f32[2,512,256]{2,1,0:T(8,128)}, f32[2,512,256]{2,1,0:T(8,128)S(1)}, u32[]{:S(2)}) copy-start(f32[2,512,256]{2,1,0:T(8,128)S(1)} %fusion.16) | copy-start | bytes 3145732
  533.9 2.7 copy-start.9
  533.9 2.7 copy-start.15
  565.6 8.5 %copy-start.32 = (f32[64,8,256]{2,1,0:T(8,128)S(1)}, f32[64,8,256]{2,1,0:T(8,128)}, u32[]{:S(2)}) copy-start(f32[64,8,256]{2,1,0:T(8,128)} %copy-done.31) | copy-start | bytes 1572868
  565.6 8.5 %copy-start.34 = (bf16[512,512]{1,0:T(8,128)(2,1)S(1)}, bf16[512,512]{1,0:T(8,128)(2,1)}, u32[]{:S(2)}) copy-start(bf16[512,512]{1,0:T(8,128)(2,1)} %param.6) | copy-start | bytes 1572868
  565.6 52.0 %all-to-all-start.9 = ((f32[2,1,512,512]{3,0,1,2:T(2,128)}), f32[2,1,512,512]{3,0,1,2:T(2,128)}, u32[]{:S(2)}, u32[]{:S(2)}) async-start(f32[2,1,512,512]{3,0,1,2:T(2,128)} %copy.152), calls=%async_computation.10 | async-start | bytes 4194304 | tf_op jit(solution)/shard_map/all_to_all | solution.py:107
  574.0 94.0 %reduce-scatter.2.cloned.1.call-start = ((), (), s32[]{:S(2)}) async-start(), calls=%async_computation.13 | async-start | bytes 5242880 | tf_op jit(solution)/shard_map/reduce_scatter | solution.py:151
  621.8 3.3 copy-start.3
  626.7 33.4 %all-to-all-start.10 = ((f32[64,8,512]{2,1,0:T(8,128)}), f32[64,8,512]{2,1,0:T(8,128)}, u32[]{:S(2)}, u32[]{:S(2)}) async-start(f32[64,8,512]{2,1,0:T(8,128)} %copy.157), calls=%async_computation.11 | async-start | bytes 2097152 | tf_op jit(solution)/shard_map/all_to_all | solution.py:111
  660.1 31.0 %all-to-all-start.11 = ((f32[64,8,512]{2,1,0:T(8,128)}), f32[64,8,512]{2,1,0:T(8,128)S(1)}, u32[]{:S(2)}, u32[]{:S(2)}) async-start(f32[64,8,512]{2,1,0:T(8,128)} %copy.160), calls=%async_computation.12 | async-start | bytes 2097152 | tf_op jit(solution)/shard_map/all_to_all | solution.py:112
  (24 other events, 41.7 us)
Sparse Core Ops, SparseCore 0:
  313.8 35.6 all-gather.1
  578.6 65.3 reduce-scatter.1
where the time goes:
time: 716 us; the launch traced here: 702 us
  waiting for transfers between devices  279 us (39%)
  matrix products  140 us (20%)
  local copies, waits for them, and re-layouts  120 us (17%)
  starting transfers between devices  99.9 us (14%)
  blocking collectives  30.6 us (4%)
  other arithmetic  17.8 us (2%)
  between operations  15.5 us (2%)
    all_to_all x2, waiting for transfers between devices, inverse_tokens(): lax.all_to_all(stacked_in, 'seq', split_axis=2, concat_axis=1, tiled=True)  63.4 us
    all_to_all x2, waiting for transfers between devices, forward_spectra(): lax.all_to_all(stacked[1], 'seq', split_axis=0, concat_axis=2, tiled=True)  53.9 us
    all_to_all x2, waiting for transfers between devices, forward_spectra(): lax.all_to_all(stacked[0], 'seq', split_axis=0, concat_axis=2, tiled=True)  53.5 us
    all_to_all x1, waiting for transfers between devices, forward_spectra(): lax.all_to_all(stacked_in, 'seq', split_axis=2, concat_axis=1, tiled=True)  47.2 us
    dot_general x8, matrix products, complex_dot(): jnp.einsum(form, table[0], operand[1], precision=HIGHEST_PREC)  34.2 us
    dot_general x8, matrix products, complex_dot(): jnp.einsum(form, table[1], operand[1], precision=HIGHEST_PREC)  33 us
    all_to_all x2, waiting for transfers between devices, inverse_tokens(): lax.all_to_all(mixed[1], 'seq', split_axis=0, concat_axis=1, tiled=True)  32.6 us
    slice x12, local copies, waits for them, and re-layouts, forward_spectra(): jnp.roll(flipped, 1, axis=0)  32.3 us
  transfers between devices with their start and end apart: 13, of which 11 were waited for; matrix products, arithmetic and copies ran while one was open for 9% of the time, Pallas kernels for 0%

commit v1 on v0

v1 whole, which is shorter than its diff:
```python
import functools
import math

import jax
import jax.numpy as jnp
import ml_dtypes
import numpy as np
from jax import lax
from jax.experimental import pallas as pl
from jax.experimental.pallas import tpu as pltpu
from jax.sharding import PartitionSpec as P

MESH = pl.DeviceIdType.MESH
F32 = jnp.float32
BF16 = jnp.bfloat16
GROUP = 8
K_SLOT, S_SLOT, D_SLOT, C_SLOT, DS_SLOT, DK_SLOT = range(6)


def split_table(table):
    high = table.astype(np.float32).astype(ml_dtypes.bfloat16)
    low = (table - high.astype(np.float64)).astype(np.float32).astype(ml_dtypes.bfloat16)
    return high, low


def make_tables(parts, rows):
    total = parts * rows
    kept = parts // 2 + 1
    padded = kept + kept % 2
    k1 = np.arange(padded)
    shard = np.arange(parts)
    pos = np.arange(rows)
    eye = np.eye(GROUP)
    angle = 2.0 * np.pi * ((k1[:, None] * shard[None, :]) % parts) / parts
    across = np.concatenate([np.kron(np.cos(angle), eye), np.kron(-np.sin(angle), eye)], 0)
    across_table = np.concatenate(split_table(across), 0)
    weight = np.where((k1 == 0) | (k1 == parts // 2), 1.0, 2.0) * (k1 < kept)
    factor = weight / (total * math.sqrt(total))
    back = np.concatenate([np.kron((np.cos(angle) * factor[:, None]).T, eye), np.kron((np.sin(angle) * factor[:, None]).T, eye)], 1)
    back_high, back_low = split_table(back)
    back_table = np.concatenate([back_high, back_high, back_low], 1)
    square = 2.0 * np.pi * ((pos[:, None] * pos[None, :]) % rows) / rows
    within = np.block([[np.cos(square), -np.sin(square)], [np.sin(square), np.cos(square)]])
    within_high, within_low = split_table(within)
    turn = 2.0 * np.pi * (k1[:, None] * pos[None, :]) / total
    turn_re = np.repeat(np.cos(turn), GROUP, 0).astype(np.float32)
    turn_im = np.repeat(-np.sin(turn), GROUP, 0).astype(np.float32)
    return across_table, within_high, within_low, back_table, turn_re, turn_im


def split_value(value):
    high = value.astype(BF16)
    return high, (value - high.astype(F32)).astype(BF16)


def kernel(
    og_ref, ig_ref, val_ref, fil_ref, w_ref, cot_ref,
    across_ref, within_hi_ref, within_lo_ref, back_ref, turn_re_ref, turn_im_ref,
    out_ref, d_og_ref, d_ig_ref, d_val_ref, d_fil_ref,
    snd, rcv, cots, d_gated, time_buf, gated, chan_buf, lhs, spec, stack,
    core_snd, core_rcv, y_snd, y_rcv, total_buf,
    snd_sem, rcv_sem, cot_snd_sem, cot_rcv_sem, red_snd_sem, red_rcv_sem,
):
    parts = lax.axis_size("seq")
    me, ch = lax.axis_index("seq"), lax.axis_index("chan")
    core, high = lax.rem(ch, 2), ch // 2
    core_peer = high * 2 + (1 - core)
    y_peer = (1 - high) * 2 + core
    far_peer = (1 - high) * 2 + (1 - core)
    rows, width = val_ref.shape
    half = rows // 2
    tile = min(128, width)
    tiles = width // tile
    groups = tile // GROUP
    msg = 2 * GROUP
    nk = turn_re_ref.shape[0]
    blk, dout = cot_ref.shape

    barrier = pltpu.get_barrier_semaphore()

    def greet(d, _):
        pl.semaphore_signal(barrier, inc=1, device_id=(lax.rem(me + d, parts), ch), device_id_type=MESH)
        return 0

    lax.fori_loop(1, parts, greet, 0)
    pl.semaphore_signal(barrier, inc=1, device_id=(me, core_peer), device_id_type=MESH)
    pl.semaphore_signal(barrier, inc=1, device_id=(me, y_peer), device_id_type=MESH)

    def message(p):
        return pl.ds(pl.multiple_of(p * msg, msg), msg)

    def send(slot):
        def go(i, _):
            p = lax.rem(me + lax.rem(i * 37, parts), parts)
            pltpu.make_async_remote_copy(
                src_ref=snd.at[slot, message(p)],
                dst_ref=rcv.at[slot, message(me)],
                send_sem=snd_sem.at[slot],
                recv_sem=rcv_sem.at[slot],
                device_id=(p, ch),
                device_id_type=MESH,
            ).start()
            return 0

        lax.fori_loop(1, parts, go, 0)
        rcv[slot, message(me)] = snd[slot, message(me)]

    def await_bytes(slot, sem):
        ref = rcv.at[slot, pl.ds(0, (parts - 1) * msg)]
        pltpu.make_async_copy(ref, ref, sem.at[slot]).wait()

    def to_messages(slot, first, second, row):
        n = first.shape[0] // GROUP
        both = jnp.concatenate([first.reshape(n, GROUP, half), second.reshape(n, GROUP, half)], 1)
        snd[slot, pl.ds(row, n * msg)] = both.reshape(n * msg, half).astype(BF16)

    def from_messages(slot, row, n):
        both = rcv[slot, pl.ds(row, n * msg)].astype(F32).reshape(n, msg, half)
        return both[:, :GROUP].reshape(n * GROUP, half), both[:, GROUP:].reshape(n * GROUP, half)

    def pack(slot, load):
        def go(t, _):
            cols = pl.ds(pl.multiple_of(t * tile, tile), tile)
            first, second = (load(pl.ds(h * half, half), cols).T for h in range(2))
            to_messages(slot, first, second, pl.multiple_of(t * groups * msg, groups * msg))
            return 0

        lax.fori_loop(0, tiles, go, 0)

    def unpack(slot, store):
        def go(t, _):
            cols = pl.ds(pl.multiple_of(t * tile, tile), tile)
            halves = from_messages(slot, pl.multiple_of(t * groups * msg, groups * msg), groups)
            for h in range(2):
                store(pl.ds(h * half, half), cols, halves[h].T)
            return 0

        lax.fori_loop(0, tiles, go, 0)

    def turn(real, imag, cols):
        a, b = turn_re_ref[:, cols], turn_im_ref[:, cols]
        return real * a - imag * b, real * b + imag * a

    def put_lhs(real, imag, cols, cols_imag):
        for value, at in ((real, cols), (imag, cols_imag)):
            hi, lo = split_value(value)
            lhs[:nk, at] = hi
            lhs[nk:, at] = lo

    def halves_of(h):
        return (
            pl.ds(pl.multiple_of(h * half, half), half),
            pl.ds(pl.multiple_of(rows + h * half, half), half),
        )

    def within(dst):
        def go(j, _):
            cols = pl.ds(pl.multiple_of(j * half, half), half)
            both = jnp.dot(lhs[...], within_hi_ref[:, cols], preferred_element_type=F32)
            rest = jnp.dot(lhs[:nk], within_lo_ref[:, cols], preferred_element_type=F32)
            spec[dst, :, cols] = both[:nk] + both[nk:] + rest
            return 0

        lax.fori_loop(0, 4, go, 0)

    def forward(slot, dst):
        step = min(16, parts)

        def regroup(i, _):
            first, second = from_messages(slot, pl.multiple_of(i * step * msg, step * msg), step)
            at = pl.ds(pl.multiple_of(i * step * GROUP, step * GROUP), step * GROUP)
            chan_buf[at, :half] = first.astype(BF16)
            chan_buf[at, half:] = second.astype(BF16)
            return 0

        lax.fori_loop(0, parts // step, regroup, 0)

        def go(h, _):
            cols, cols_imag = halves_of(h)
            y = jnp.dot(across_ref[...], chan_buf[:, cols], preferred_element_type=F32)
            y = y[: 2 * nk] + y[2 * nk :]
            real, imag = turn(y[:nk], y[nk:], cols)
            put_lhs(real, imag, cols, cols_imag)
            return 0

        lax.fori_loop(0, 2, go, 0)
        within(dst)

    def inverse(slot, product):
        def fill(h, _):
            cols, cols_imag = halves_of(h)
            real, imag = product(cols, cols_imag)
            put_lhs(real, imag, cols, cols_imag)
            return 0

        lax.fori_loop(0, 2, fill, 0)
        within(3)

        def go(h, _):
            cols, cols_imag = halves_of(h)
            real, imag = turn(spec[3, :, cols], spec[3, :, cols_imag], cols)
            for i, value in enumerate((real, imag)):
                hi, lo = split_value(value)
                stack[i * nk : (i + 1) * nk, cols] = hi
                stack[(2 + i) * nk : (3 + i) * nk, cols] = lo
                stack[(4 + i) * nk : (5 + i) * nk, cols] = hi
            time_buf[:, cols] = jnp.dot(back_ref[...], stack[:, cols], preferred_element_type=F32)
            return 0

        lax.fori_loop(0, 2, go, 0)
        step = min(16, parts)

        def regroup(i, _):
            at = pl.ds(pl.multiple_of(i * step * GROUP, step * GROUP), step * GROUP)
            to_messages(slot, time_buf[at, :half], time_buf[at, half:], pl.multiple_of(i * step * msg, step * msg))
            return 0

        lax.fori_loop(0, parts // step, regroup, 0)
        send(slot)

    pack(K_SLOT, lambda r, c: fil_ref[r, c].astype(F32))
    pl.semaphore_wait(barrier, parts + 1)

    def to_chan(i, src, dst, peer, snd_sems, rcv_sems):
        return pltpu.make_async_remote_copy(
            src_ref=src, dst_ref=dst, send_sem=snd_sems.at[i], recv_sem=rcv_sems.at[i],
            device_id=(me, peer), device_id_type=MESH,
        )

    cot_y = to_chan(0, cot_ref, cots.at[ch], y_peer, cot_snd_sem, cot_rcv_sem)
    cot_core = to_chan(1, cot_ref, cots.at[ch], core_peer, cot_snd_sem, cot_rcv_sem)
    cot_y.start()
    cot_core.start()
    send(K_SLOT)
    pack(S_SLOT, lambda r, c: ig_ref[r, c].astype(F32) * val_ref[r, c].astype(F32))
    send(S_SLOT)

    def d_block(block_ref, b):
        at = pl.ds(pl.multiple_of(b * blk, blk), blk)
        d = lax.dot_general(block_ref[...], w_ref[...], (((1,), (1,)), ((), ())), preferred_element_type=F32)
        d_gated[at] = d
        time_buf[at] = d * og_ref[at].astype(F32)

    d_block(cot_ref, ch)
    cot_y.wait_recv()
    cot_far = to_chan(2, cots.at[y_peer], cots.at[y_peer], core_peer, cot_snd_sem, cot_rcv_sem)
    cot_far.start()
    d_block(cots.at[y_peer], y_peer)
    cot_core.wait_recv()
    d_block(cots.at[core_peer], core_peer)
    cot_far.wait_recv()
    d_block(cots.at[far_peer], far_peer)
    pack(D_SLOT, lambda r, c: time_buf[r, c])
    send(D_SLOT)

    await_bytes(K_SLOT, rcv_sem)
    forward(K_SLOT, 0)
    await_bytes(S_SLOT, rcv_sem)
    forward(S_SLOT, 1)

    def conv_product(cols, cols_imag):
        a, b = spec[0, :, cols], spec[0, :, cols_imag]
        c, d = spec[1, :, cols], spec[1, :, cols_imag]
        return a * c - b * d, -(a * d + b * c)

    inverse(C_SLOT, conv_product)
    await_bytes(D_SLOT, rcv_sem)
    forward(D_SLOT, 2)

    def correlation(which):
        def product(cols, cols_imag):
            a, b = spec[which, :, cols], spec[which, :, cols_imag]
            c, d = spec[2, :, cols], spec[2, :, cols_imag]
            return a * c + b * d, b * c - a * d

        return product

    inverse(DS_SLOT, correlation(0))
    inverse(DK_SLOT, correlation(1))

    await_bytes(C_SLOT, rcv_sem)

    def use_conv(r, c, conv):
        gated[r, c] = (og_ref[r, c].astype(F32) * conv).astype(BF16)
        d_og_ref[r, c] = d_gated[r, c] * conv

    unpack(C_SLOT, use_conv)
    out_tile = min(512, dout)

    def project(of_core, store):
        for j in range(2):
            at = pl.ds(pl.multiple_of((2 * j + of_core) * blk, blk), blk)

            def go(n, _, j=j, at=at):
                cols = pl.ds(pl.multiple_of(n * out_tile, out_tile), out_tile)
                store(j, cols, jnp.dot(gated[at], w_ref[:, cols], preferred_element_type=F32))
                return 0

            lax.fori_loop(0, dout // out_tile, go, 0)

    def store_peer(j, cols, value):
        core_snd[j, :, cols] = value.astype(BF16)

    def store_mine(j, cols, value):
        total_buf[j, :, cols] = value

    project(1 - core, store_peer)
    red_core = to_chan(0, core_snd, core_rcv, core_peer, red_snd_sem, red_rcv_sem)
    red_core.start()
    project(core, store_mine)
    red_core.wait_recv()
    y_snd[...] = (total_buf[1 - high] + core_rcv[1 - high].astype(F32)).astype(BF16)
    red_y = to_chan(1, y_snd, y_rcv, y_peer, red_snd_sem, red_rcv_sem)
    red_y.start()
    total_buf[high] = total_buf[high] + core_rcv[high].astype(F32)
    red_y.wait_recv()
    out_ref[...] = (total_buf[high] + y_rcv[...].astype(F32)).astype(BF16)

    await_bytes(DS_SLOT, rcv_sem)

    def use_source(r, c, grad):
        d_ig_ref[r, c] = grad * val_ref[r, c].astype(F32)
        d_val_ref[r, c] = grad * ig_ref[r, c].astype(F32)

    unpack(DS_SLOT, use_source)
    await_bytes(DK_SLOT, rcv_sem)

    def use_kernel(r, c, grad):
        d_fil_ref[r, c] = grad

    unpack(DK_SLOT, use_kernel)

    for slot in range(6):
        await_bytes(slot, snd_sem)
    for copy in (cot_y, cot_core, cot_far, red_core, red_y):
        copy.wait_send()


def on_device(out_gate, in_gate, values, filter_param, out_weight, out_cotangent):
    rows, width = values.shape
    parts = lax.axis_size("seq")
    blk, dout = out_cotangent.shape
    tables = make_tables(parts, rows)
    nk = tables[4].shape[0]
    msgs = (parts * 2 * GROUP, rows // 2)
    vmem = pl.BlockSpec(memory_space=pltpu.VMEM)
    grad = jax.ShapeDtypeStruct((rows, width), F32)
    return pl.pallas_call(
        kernel,
        out_shape=(jax.ShapeDtypeStruct((blk, dout), BF16), grad, grad, grad, grad),
        in_specs=[vmem] * 12,
        out_specs=(vmem,) * 5,
        scratch_shapes=[
            pltpu.VMEM((6, *msgs), BF16),
            pltpu.VMEM((6, *msgs), BF16),
            pltpu.VMEM((4, blk, dout), BF16),
            pltpu.VMEM((rows, width), F32),
            pltpu.VMEM((rows, width), F32),
            pltpu.VMEM((rows, width), BF16),
            pltpu.VMEM((parts * GROUP, rows), BF16),
            pltpu.VMEM((2 * nk, 2 * rows), BF16),
            pltpu.VMEM((4, nk, 2 * rows), F32),
            pltpu.VMEM((6 * nk, rows), BF16),
            pltpu.VMEM((2, blk, dout), BF16),
            pltpu.VMEM((2, blk, dout), BF16),
            pltpu.VMEM((blk, dout), BF16),
            pltpu.VMEM((blk, dout), BF16),
            pltpu.VMEM((2, blk, dout), F32),
            pltpu.SemaphoreType.DMA((6,)),
            pltpu.SemaphoreType.DMA((6,)),
            pltpu.SemaphoreType.DMA((3,)),
            pltpu.SemaphoreType.DMA((3,)),
            pltpu.SemaphoreType.DMA((2,)),
            pltpu.SemaphoreType.DMA((2,)),
        ],
        compiler_params=pltpu.CompilerParams(collective_id=0, has_side_effects=True, vmem_limit_bytes=60 * 2**20),
    )(out_gate, in_gate, values, filter_param, out_weight, out_cotangent, *tables)


def solution(mesh):
    return jax.shard_map(
        on_device,
        mesh=mesh,
        in_specs=(
            P("seq", "chan"),
            P("seq", "chan"),
            P("seq", "chan"),
            P("seq", "chan"),
            P("chan", None),
            P(("seq", "chan"), None),
        ),
        out_specs=(
            P(("seq", "chan"), None),
            P("seq", "chan"),
            P("seq", "chan"),
            P("seq", "chan"),
            P("seq", "chan"),
        ),
        check_vma=False,
    )
```

time: 716 us -> 108 us (0.15); the launches traced: 702 us -> 108 us
  waiting for transfers between devices: 279 us -> 0 us
  matrix products: 140 us -> 0 us
  local copies, waits for them, and re-layouts: 120 us -> 7.24 us
  Pallas kernels: 0 us -> 100 us
  starting transfers between devices: 99.9 us -> 0 us
  blocking collectives: 30.6 us -> 0 us
  other arithmetic: 17.8 us -> 0 us
  between operations: 15.5 us -> 0.65 us
    all_to_all x11 -> x0, waiting for transfers between devices: 278 us -> none  [the longest x2 63.4 us: inverse_tokens(): lax.all_to_all(stacked_in, 'seq', split_axis=2, concat_axis=1, tiled=True)]
    dot_general x34 -> x0, matrix products: 140 us -> none  [the longest x8 34.2 us: complex_dot(): jnp.einsum(form, table[0], operand[1], precision=HIGHEST_PREC)]
    pallas_call x0 -> x1, Pallas kernels: none -> 100 us  [on_device(): pl.pallas_call(kernel, out_shape=(jax.ShapeDtypeStruct((blk, dout), BF16)...]
    all_to_all x11 -> x0, starting transfers between devices: 99.6 us -> none  [the longest x2 18.3 us: inverse_tokens(): lax.all_to_all(mixed[0], 'seq', split_axis=0, concat_axis=1, tiled=True)]
    slice x44 -> x0, local copies, waits for them, and re-layouts: 61.8 us -> none  [the longest x12 32.3 us: forward_spectra(): jnp.roll(flipped, 1, axis=0)]
    all_to_all x1 -> x0, blocking collectives: 30.6 us -> none  [forward_spectra(): lax.all_to_all(stacked_in, 'seq', split_axis=2, concat_axis=1, tiled=True)]
    rev x4 -> x0, local copies, waits for them, and re-layouts: 25.3 us -> none  [the longest x2 13.7 us: forward_spectra(): source[1][::-1]]
    mul x8 -> x0, other arithmetic: 11.7 us -> none  [the longest x2 4.06 us: forward_spectra(): first = (0.5 * (own[0] + mirrored[0]), 0.5 * (own[1] - mirrored[1]))]
  transfers between devices with their start and end apart: 13 -> 0, of which waited for: 11 -> 0; matrix products, arithmetic and copies ran while one was open for 9% -> 0% of each run, Pallas kernels for 0% -> 0%
where the time goes in v1:
time: 108 us
  Pallas kernels  100 us (93%)
  local copies, waits for them, and re-layouts  7.24 us (7%)
    pallas_call x1, Pallas kernels, on_device(): pl.pallas_call(kernel, out_shape=(jax.ShapeDtypeStruct((blk, dout), BF16)...  100 us
    unnamed x11, local copies, waits for them, and re-layouts  7.24 us

profile of v1, /device:TPU:1, one launch (start us, length us, event | category | flops | bytes accessed | tf_op | source)
XLA Modules:
  0.0 108.3 jit_solution(9717313424590068415)
XLA Ops:
  0.6 100.4 %shard_map.155 = (bf16[128,2048]{1,0:T(8,128)(2,1)}, f32[512,512]{1,0:T(8,128)}, f32[512,512]{1,0:T(8,128)}, f32[512,512]{1,0:T(8,128)}, f32[512,512]{1,0:T(8,128)}) custom-call(bf16[512,512]{1,0:T(8,128)(2,1)} %og_ref.1, bf16[512,512]{1,0:T(8,128)(2,1)} %ig_ref.1, bf16[512,512]{1,0:T(8,128)(2,1)} %val_ref.1, bf16[512,512]{1,0:T(8,128)(2,1)} %fil_ref.1, ...), custom_call_target="tpu_custom_call" | custom-call | tf_op jit(solution)/shard_map/pallas_call | solution.py:348
  101.0 0.0 copy-start.2
  101.1 2.0 %copy.22 = bf16[128,2048]{1,0:T(8,128)(2,1)} copy(bf16[128,2048]{1,0:T(8,128)(2,1)} %get-tuple-element.10) | data formatting | bytes 1048576
  103.0 0.0 copy-start.1
  103.0 2.4 %copy.23 = f32[512,512]{1,0:T(8,128)} copy(f32[512,512]{1,0:T(8,128)} %get-tuple-element.11) | data formatting | bytes 2097152
  105.4 0.0 copy-done.2
  105.4 0.0 copy-start
  105.4 1.0 copy.24
  106.3 0.0 copy-done.1
  106.4 1.0 copy.25
  107.3 0.0 copy-done
  107.3 1.0 copy.26
Async XLA Ops:
  101.0 4.3 %copy-start.2 = (f32[512,512]{1,0:T(8,128)S(1)}, f32[512,512]{1,0:T(8,128)}, u32[]{:S(2)}) copy-start(f32[512,512]{1,0:T(8,128)} %get-tuple-element.12) | copy-start | bytes 3145732
  103.0 3.3 %copy-start.1 = (f32[512,512]{1,0:T(8,128)S(1)}, f32[512,512]{1,0:T(8,128)}, u32[]{:S(2)}) copy-start(f32[512,512]{1,0:T(8,128)} %get-tuple-element.13) | copy-start | bytes 3145732
  105.4 1.9 %copy-start = (f32[512,512]{1,0:T(8,128)S(1)}, f32[512,512]{1,0:T(8,128)}, u32[]{:S(2)}) copy-start(f32[512,512]{1,0:T(8,128)} %get-tuple-element.14) | copy-start | bytes 3145732

commit v2 on v1

v2 whole, which is shorter than its diff:
```python
import functools
import math

import jax
import jax.numpy as jnp
import ml_dtypes
import numpy as np
from jax import lax
from jax.experimental import pallas as pl
from jax.experimental.pallas import tpu as pltpu
from jax.sharding import PartitionSpec as P

MESH = pl.DeviceIdType.MESH
F32 = jnp.float32
BF16 = jnp.bfloat16
GROUP = 8
TILE = 128
K_SLOT, S_SLOT, D_SLOT, C_SLOT, DS_SLOT, DK_SLOT = range(6)


def split_table(table):
    high = table.astype(np.float32).astype(ml_dtypes.bfloat16)
    low = (table - high.astype(np.float64)).astype(np.float32).astype(ml_dtypes.bfloat16)
    return high, low


def make_tables(parts, rows):
    total = parts * rows
    kept = parts // 2 + 1
    padded = kept + kept % 2
    k1 = np.arange(padded)
    shard = np.arange(parts)
    pos = np.arange(rows)
    eye = np.eye(GROUP)
    angle = 2.0 * np.pi * ((k1[:, None] * shard[None, :]) % parts) / parts
    across = np.concatenate([np.kron(np.cos(angle), eye), np.kron(-np.sin(angle), eye)], 0)
    across_table = np.concatenate(split_table(across), 0)
    weight = np.where((k1 == 0) | (k1 == parts // 2), 1.0, 2.0) * (k1 < kept)
    factor = weight / (total * math.sqrt(total))
    back = np.concatenate([np.kron((np.cos(angle) * factor[:, None]).T, eye), np.kron((np.sin(angle) * factor[:, None]).T, eye)], 1)
    back_high, back_low = split_table(back)
    back_table = np.concatenate([back_high, back_high, back_low], 1)
    square = 2.0 * np.pi * ((pos[:, None] * pos[None, :]) % rows) / rows
    within = np.block([[np.cos(square), -np.sin(square)], [np.sin(square), np.cos(square)]])
    within_high, within_low = split_table(within)
    turn = 2.0 * np.pi * (k1[:, None] * pos[None, :]) / total
    turn_re = np.repeat(np.cos(turn), GROUP, 0).astype(np.float32)
    turn_im = np.repeat(-np.sin(turn), GROUP, 0).astype(np.float32)
    return across_table, within_high, within_low, back_table, turn_re, turn_im


def split_value(value):
    high = value.astype(BF16)
    return high, (value - high.astype(F32)).astype(BF16)


def kernel(
    og_hbm, ig_hbm, val_hbm, fil_hbm, w_hbm, cot_hbm,
    across_hbm, within_hi_hbm, within_lo_hbm, back_hbm, turn_re_hbm, turn_im_hbm,
    out_hbm, d_og_hbm, ds_hbm, dk_hbm,
    og_ref, ig_ref, val_ref, fil_ref, w_ref,
    across_ref, within_hi_ref, within_lo_ref, back_ref, turn_re_ref, turn_im_ref,
    snd, rcv, cots, d_gated, time_buf, gated, d_og_buf, chan_buf, lhs, spec, stack,
    core_snd, core_rcv, y_snd, y_rcv, total_buf, out_buf,
    load_sem, store_sem, snd_sem, rcv_sem, cot_snd_sem, cot_rcv_sem, red_snd_sem, red_rcv_sem,
):
    parts = lax.axis_size("seq")
    me, ch = lax.axis_index("seq"), lax.axis_index("chan")
    core, high = lax.rem(ch, 2), ch // 2
    core_peer = high * 2 + (1 - core)
    y_peer = (1 - high) * 2 + core
    far_peer = (1 - high) * 2 + (1 - core)
    rows, width = val_ref.shape
    half = rows // 2
    tile = min(TILE, width)
    tiles = width // tile
    groups = tile // GROUP
    msg = 2 * GROUP
    nk = turn_re_ref.shape[0]
    _, blk, dout = cots.shape
    my_tile, my_group = lax.rem(me, tiles), me // tiles
    my_slot = my_tile * groups + my_group

    loads = {}
    for i, (name, src, dst) in enumerate(
        (
            ("cot", cot_hbm, cots.at[ch]),
            ("fil", fil_hbm, fil_ref),
            ("ig", ig_hbm, ig_ref),
            ("val", val_hbm, val_ref),
            ("w", w_hbm, w_ref),
            ("og", og_hbm, og_ref),
            ("across", across_hbm, across_ref),
            ("turn_re", turn_re_hbm, turn_re_ref),
            ("turn_im", turn_im_hbm, turn_im_ref),
            ("within_hi", within_hi_hbm, within_hi_ref),
            ("within_lo", within_lo_hbm, within_lo_ref),
            ("back", back_hbm, back_ref),
        )
    ):
        loads[name] = pltpu.make_async_copy(src, dst, load_sem.at[i])
        loads[name].start()

    def loaded(*names):
        for name in names:
            loads[name].wait()

    barrier = pltpu.get_barrier_semaphore()

    def greet(d, _):
        pl.semaphore_signal(barrier, inc=1, device_id=(lax.rem(me + d, parts), ch), device_id_type=MESH)
        return 0

    pl.semaphore_signal(barrier, inc=1, device_id=(me, core_peer), device_id_type=MESH)
    pl.semaphore_signal(barrier, inc=1, device_id=(me, y_peer), device_id_type=MESH)
    lax.fori_loop(1, parts, greet, 0)

    def message(p):
        return pl.ds(pl.multiple_of(p * msg, msg), msg)

    def send_one(slot, src_slot, dst, p):
        pltpu.make_async_remote_copy(
            src_ref=snd.at[slot, message(src_slot)],
            dst_ref=dst,
            send_sem=snd_sem.at[slot],
            recv_sem=rcv_sem.at[slot],
            device_id=(p, ch),
            device_id_type=MESH,
        ).start()

    def send_back(slot, dst):
        def go(i, _):
            p = lax.rem(me + lax.rem(i * 37, parts), parts)
            send_one(slot, p, dst, p)
            return 0

        lax.fori_loop(1, parts, go, 0)

    def await_bytes(ref, sem):
        ref = ref.at[pl.ds(0, (parts - 1) * msg)]
        pltpu.make_async_copy(ref, ref, sem).wait()

    def arrived(slot):
        await_bytes(rcv.at[slot], rcv_sem.at[slot])

    def to_messages(slot, first, second, row):
        n = first.shape[0] // GROUP
        both = jnp.concatenate([first.reshape(n, GROUP, half), second.reshape(n, GROUP, half)], 1)
        snd[slot, pl.ds(row, n * msg)] = both.reshape(n * msg, half).astype(BF16)

    def send_tile(slot, load, u):
        t = lax.rem(my_tile + u, tiles)
        cols = pl.ds(pl.multiple_of(t * tile, tile), tile)
        first, second = (load(pl.ds(h * half, half), cols).T for h in range(2))
        to_messages(slot, first, second, pl.multiple_of(t * groups * msg, groups * msg))

        def go(i, _):
            j = lax.rem(my_group + i, groups)
            send_one(slot, t * groups + j, rcv.at[slot, message(me)], j * tiles + t)
            return 0

        lax.fori_loop(jnp.maximum(1 - u, 0), groups, go, 0)

    def send_tiles(slot, load, start, stop):
        def go(u, _):
            send_tile(slot, load, u)
            return 0

        lax.fori_loop(start, stop, go, 0)
        if start == 0:
            rcv[slot, message(me)] = snd[slot, message(my_slot)]

    def turn(real, imag, cols):
        a, b = turn_re_ref[:, cols], turn_im_ref[:, cols]
        return real * a - imag * b, real * b + imag * a

    def put_lhs(real, imag, cols, cols_imag):
        for value, at in ((real, cols), (imag, cols_imag)):
            hi, lo = split_value(value)
            lhs[:nk, at] = hi
            lhs[nk:, at] = lo

    def halves_of(h):
        return (
            pl.ds(pl.multiple_of(h * half, half), half),
            pl.ds(pl.multiple_of(rows + h * half, half), half),
        )

    def within(dst):
        def go(j, _):
            cols = pl.ds(pl.multiple_of(j * half, half), half)
            both = jnp.dot(lhs[...], within_hi_ref[:, cols], preferred_element_type=F32)
            rest = jnp.dot(lhs[:nk], within_lo_ref[:, cols], preferred_element_type=F32)
            spec[dst, :, cols] = both[:nk] + both[nk:] + rest
            return 0

        lax.fori_loop(0, 4, go, 0)

    step = min(16, parts)

    def forward(slot, dst):
        def regroup(i, _):
            both = rcv[slot, pl.ds(pl.multiple_of(i * step * msg, step * msg), step * msg)]
            both = both.astype(F32).reshape(step, msg, half)
            at = pl.ds(pl.multiple_of(i * step * GROUP, step * GROUP), step * GROUP)
            chan_buf[at, :half] = both[:, :GROUP].reshape(step * GROUP, half).astype(BF16)
            chan_buf[at, half:] = both[:, GROUP:].reshape(step * GROUP, half).astype(BF16)
            return 0

        lax.fori_loop(0, parts // step, regroup, 0)

        def go(h, _):
            cols, cols_imag = halves_of(h)
            y = jnp.dot(across_ref[...], chan_buf[:, cols], preferred_element_type=F32)
            y = y[: 2 * nk] + y[2 * nk :]
            real, imag = turn(y[:nk], y[nk:], cols)
            put_lhs(real, imag, cols, cols_imag)
            return 0

        lax.fori_loop(0, 2, go, 0)
        within(dst)

    def inverse(slot, product):
        def fill(h, _):
            cols, cols_imag = halves_of(h)
            real, imag = product(cols, cols_imag)
            put_lhs(real, imag, cols, cols_imag)
            return 0

        lax.fori_loop(0, 2, fill, 0)
        within(3)

        def go(h, _):
            cols, cols_imag = halves_of(h)
            real, imag = turn(spec[3, :, cols], spec[3, :, cols_imag], cols)
            for i, value in enumerate((real, imag)):
                hi, lo = split_value(value)
                stack[i * nk : (i + 1) * nk, cols] = hi
                stack[(2 + i) * nk : (3 + i) * nk, cols] = lo
                stack[(4 + i) * nk : (5 + i) * nk, cols] = hi
            time_buf[:, cols] = jnp.dot(back_ref[...], stack[:, cols], preferred_element_type=F32)
            return 0

        lax.fori_loop(0, 2, go, 0)

        def regroup(i, _):
            at = pl.ds(pl.multiple_of(i * step * GROUP, step * GROUP), step * GROUP)
            to_messages(slot, time_buf[at, :half], time_buf[at, half:], pl.multiple_of(i * step * msg, step * msg))
            return 0

        lax.fori_loop(0, parts // step, regroup, 0)

    def to_chan(i, src, dst, peer, snd_sems, rcv_sems):
        return pltpu.make_async_remote_copy(
            src_ref=src, dst_ref=dst, send_sem=snd_sems.at[i], recv_sem=rcv_sems.at[i],
            device_id=(me, peer), device_id_type=MESH,
        )

    def cot_copy(i, owner, h, peer):
        ref = cots.at[owner, pl.ds(h * (blk // 2), blk // 2)]
        return to_chan(i, ref, ref, peer, cot_snd_sem, cot_rcv_sem)

    cot_y = [cot_copy(h, ch, h, y_peer) for h in range(2)]
    cot_core = to_chan(2, cots.at[ch], cots.at[ch], core_peer, cot_snd_sem, cot_rcv_sem)
    cot_far = [cot_copy(3 + h, y_peer, h, core_peer) for h in range(2)]

    loaded("cot", "fil")
    pl.semaphore_wait(barrier, parts + 1)
    cot_y[0].start()
    cot_y[1].start()
    cot_core.start()
    send_tiles(K_SLOT, lambda r, c: fil_ref[r, c].astype(F32), 0, tiles)
    loaded("ig", "val")

    def source(r, c):
        return ig_ref[r, c].astype(F32) * val_ref[r, c].astype(F32)

    send_tiles(S_SLOT, source, 0, tiles // 2)
    loaded("w", "og")

    def d_block(b):
        at = pl.ds(pl.multiple_of(b * blk, blk), blk)
        d = lax.dot_general(cots[b], w_ref[...], (((1,), (1,)), ((), ())), preferred_element_type=F32)
        d_gated[at] = d
        time_buf[at] = d * og_ref[at].astype(F32)

    d_block(ch)
    for h in range(2):
        cot_y[h].wait_recv()
        cot_far[h].start()
    send_tiles(S_SLOT, source, tiles // 2, tiles)
    d_block(y_peer)
    cot_core.wait_recv()
    d_block(core_peer)
    cot_far[0].wait_recv()
    cot_far[1].wait_recv()
    d_block(far_peer)
    send_tiles(D_SLOT, lambda r, c: time_buf[r, c], 0, tiles)

    loaded("across", "turn_re", "turn_im", "within_hi", "within_lo", "back")
    arrived(K_SLOT)
    forward(K_SLOT, 0)
    arrived(S_SLOT)
    forward(S_SLOT, 1)

    def conv_product(cols, cols_imag):
        a, b = spec[0, :, cols], spec[0, :, cols_imag]
        c, d = spec[1, :, cols], spec[1, :, cols_imag]
        return a * c - b * d, -(a * d + b * c)

    inverse(C_SLOT, conv_product)
    send_back(C_SLOT, rcv.at[C_SLOT, message(my_slot)])
    rcv[C_SLOT, message(my_slot)] = snd[C_SLOT, message(me)]
    arrived(D_SLOT)
    forward(D_SLOT, 2)

    def correlation(which):
        def product(cols, cols_imag):
            a, b = spec[which, :, cols], spec[which, :, cols_imag]
            c, d = spec[2, :, cols], spec[2, :, cols_imag]
            return a * c + b * d, b * c - a * d

        return product

    inverse(DS_SLOT, correlation(0))
    send_back(DS_SLOT, ds_hbm.at[message(my_slot)])
    own_ds = pltpu.make_async_copy(snd.at[DS_SLOT, message(me)], ds_hbm.at[message(my_slot)], store_sem.at[0])
    own_ds.start()
    inverse(DK_SLOT, correlation(1))
    own_dk = pltpu.make_async_copy(snd.at[DK_SLOT, message(me)], dk_hbm.at[message(my_slot)], store_sem.at[1])
    own_dk.start()

    arrived(C_SLOT)

    def use_conv(t, _):
        cols = pl.ds(pl.multiple_of(t * tile, tile), tile)
        both = rcv[C_SLOT, pl.ds(pl.multiple_of(t * groups * msg, groups * msg), groups * msg)]
        both = both.astype(F32).reshape(groups, msg, half)
        for h in range(2):
            conv = both[:, h * GROUP : (h + 1) * GROUP].reshape(tile, half).T
            at = pl.ds(h * half, half)
            gated[at, cols] = (og_ref[at, cols].astype(F32) * conv).astype(BF16)
            d_og_buf[at, cols] = d_gated[at, cols] * conv
        return 0

    lax.fori_loop(0, tiles, use_conv, 0)
    d_og_out = pltpu.make_async_copy(d_og_buf, d_og_hbm, store_sem.at[2])
    d_og_out.start()
    out_tile = min(512, dout)

    def project(j, of_core, store):
        at = pl.ds(pl.multiple_of((2 * j + of_core) * blk, blk), blk)

        def go(n, _):
            cols = pl.ds(pl.multiple_of(n * out_tile, out_tile), out_tile)
            store(cols, jnp.dot(gated[at], w_ref[:, cols], preferred_element_type=F32))
            return 0

        lax.fori_loop(0, dout // out_tile, go, 0)

    def store_peer(i):
        def store(cols, value):
            core_snd[i, :, cols] = value.astype(BF16)

        return store

    def store_mine(i):
        def store(cols, value):
            total_buf[i, :, cols] = value

        return store

    red_core = [to_chan(i, core_snd.at[i], core_rcv.at[i], core_peer, red_snd_sem, red_rcv_sem) for i in range(2)]
    red_y = to_chan(2, y_snd, y_rcv, y_peer, red_snd_sem, red_rcv_sem)
    project(1 - high, 1 - core, store_peer(0))
    red_core[0].start()
    project(1 - high, core, store_mine(0))
    red_core[0].wait_recv()
    y_snd[...] = (total_buf[0] + core_rcv[0].astype(F32)).astype(BF16)
    red_y.start()
    project(high, 1 - core, store_peer(1))
    red_core[1].start()
    send_back(DK_SLOT, dk_hbm.at[message(my_slot)])
    project(high, core, store_mine(1))
    red_core[1].wait_recv()
    total_buf[1] = total_buf[1] + core_rcv[1].astype(F32)
    red_y.wait_recv()
    out_buf[...] = (total_buf[1] + y_rcv[...].astype(F32)).astype(BF16)
    out_out = pltpu.make_async_copy(out_buf, out_hbm, store_sem.at[3])
    out_out.start()

    await_bytes(ds_hbm, rcv_sem.at[DS_SLOT])
    for slot in range(6):
        await_bytes(snd.at[slot], snd_sem.at[slot])
    for copy in (*cot_y, cot_core, *cot_far, *red_core, red_y):
        copy.wait_send()
    for copy in (own_ds, own_dk, d_og_out, out_out):
        copy.wait()
    await_bytes(dk_hbm, rcv_sem.at[DK_SLOT])


def finish(ig_ref, val_ref, ds_ref, dk_ref, d_og_in, out_in, d_ig_ref, d_val_ref, d_fil_ref, d_og_ref, out_ref):
    rows, tile = val_ref.shape
    half = rows // 2
    groups = tile // GROUP

    def positions(ref, h):
        both = ref[...].astype(F32).reshape(groups, 2 * GROUP, half)
        return both[:, h * GROUP : (h + 1) * GROUP].reshape(tile, half).T

    for h in range(2):
        at = pl.ds(h * half, half)
        grad = positions(ds_ref, h)
        d_ig_ref[at] = grad * val_ref[at].astype(F32)
        d_val_ref[at] = grad * ig_ref[at].astype(F32)
        d_fil_ref[at] = positions(dk_ref, h)
    d_og_ref[...] = d_og_in[...]
    out_ref[...] = out_in[...]


def on_device(out_gate, in_gate, values, filter_param, out_weight, out_cotangent):
    rows, width = values.shape
    parts = lax.axis_size("seq")
    blk, dout = out_cotangent.shape
    tables = make_tables(parts, rows)
    nk = tables[4].shape[0]
    msgs = (parts * 2 * GROUP, rows // 2)
    tile = min(TILE, width)
    tiles = width // tile
    operands = (out_gate, in_gate, values, filter_param, out_weight, out_cotangent, *tables)
    grad = jax.ShapeDtypeStruct((rows, width), F32)
    block_out = jax.ShapeDtypeStruct((blk, dout), BF16)
    raw = jax.ShapeDtypeStruct(msgs, BF16)
    anywhere = pl.BlockSpec(memory_space=pl.ANY)
    output, d_og, ds_raw, dk_raw = pl.pallas_call(
        kernel,
        out_shape=(block_out, grad, raw, raw),
        in_specs=[anywhere] * 12,
        out_specs=(anywhere,) * 4,
        scratch_shapes=[
            *(pltpu.VMEM(x.shape, x.dtype) for i, x in enumerate(operands) if i != 5),
            pltpu.VMEM((6, *msgs), BF16),
            pltpu.VMEM((4, *msgs), BF16),
            pltpu.VMEM((4, blk, dout), BF16),
            pltpu.VMEM((rows, width), F32),
            pltpu.VMEM((rows, width), F32),
            pltpu.VMEM((rows, width), BF16),
            pltpu.VMEM((rows, width), F32),
            pltpu.VMEM((parts * GROUP, rows), BF16),
            pltpu.VMEM((2 * nk, 2 * rows), BF16),
            pltpu.VMEM((4, nk, 2 * rows), F32),
            pltpu.VMEM((6 * nk, rows), BF16),
            pltpu.VMEM((2, blk, dout), BF16),
            pltpu.VMEM((2, blk, dout), BF16),
            pltpu.VMEM((blk, dout), BF16),
            pltpu.VMEM((blk, dout), BF16),
            pltpu.VMEM((2, blk, dout), F32),
            pltpu.VMEM((blk, dout), BF16),
            pltpu.SemaphoreType.DMA((12,)),
            pltpu.SemaphoreType.DMA((4,)),
            pltpu.SemaphoreType.DMA((6,)),
            pltpu.SemaphoreType.DMA((6,)),
            pltpu.SemaphoreType.DMA((5,)),
            pltpu.SemaphoreType.DMA((5,)),
            pltpu.SemaphoreType.DMA((3,)),
            pltpu.SemaphoreType.DMA((3,)),
        ],
        compiler_params=pltpu.CompilerParams(collective_id=0, has_side_effects=True, vmem_limit_bytes=60 * 2**20),
    )(*operands)
    by_channel = pl.BlockSpec((rows, tile), lambda t: (0, t))
    by_row = pl.BlockSpec((msgs[0] // tiles, msgs[1]), lambda t: (t, 0))
    out_rows = pl.BlockSpec((blk // tiles, dout), lambda t: (t, 0))
    d_ig, d_val, d_fil, d_og, output = pl.pallas_call(
        finish,
        grid=(tiles,),
        out_shape=(grad, grad, grad, grad, block_out),
        in_specs=[by_channel, by_channel, by_row, by_row, by_channel, out_rows],
        out_specs=(by_channel, by_channel, by_channel, by_channel, out_rows),
        compiler_params=pltpu.CompilerParams(vmem_limit_bytes=40 * 2**20),
    )(in_gate, values, ds_raw, dk_raw, d_og, output)
    return output, d_og, d_ig, d_val, d_fil


def solution(mesh):
    return jax.shard_map(
        on_device,
        mesh=mesh,
        in_specs=(
            P("seq", "chan"),
            P("seq", "chan"),
            P("seq", "chan"),
            P("seq", "chan"),
            P("chan", None),
            P(("seq", "chan"), None),
        ),
        out_specs=(
            P(("seq", "chan"), None),
            P("seq", "chan"),
            P("seq", "chan"),
            P("seq", "chan"),
            P("seq", "chan"),
        ),
        check_vma=False,
    )
```

time: 108 us -> 100 us (0.926)
  Pallas kernels: 100 us -> 95 us
  local copies, waits for them, and re-layouts: 7.24 us -> 4.35 us
    pallas_call x1 -> x2, Pallas kernels: 100 us -> 95 us  [the longest x1 92.1 us: on_device(): pl.pallas_call(kernel, out_shape=(block_out, grad, raw, raw), in_specs=[a...]
    unnamed x11 -> x12, local copies, waits for them, and re-layouts: 7.24 us -> 4.35 us
where the time goes in v2:
time: 100 us
  Pallas kernels  95 us (95%)
  local copies, waits for them, and re-layouts  4.35 us (4%)
    pallas_call x1, Pallas kernels, on_device(): pl.pallas_call(kernel, out_shape=(block_out, grad, raw, raw), in_specs=[a...  92.1 us
    unnamed x12, local copies, waits for them, and re-layouts  4.35 us
    pallas_call x1, Pallas kernels, on_device(): pl.pallas_call(finish, grid=(tiles,), out_shape=(grad, grad, grad, grad,...  2.87 us

profile of v2, /device:TPU:1, one launch (start us, length us, event | category | flops | bytes accessed | tf_op | source)
XLA Modules:
  0.0 100.0 jit_solution(16341019037903285839)
XLA Ops:
  0.6 0.0 copy-start.1
  0.6 0.0 copy-start
  0.7 92.1 %shard_map.155 = (bf16[128,2048]{1,0:T(8,128)(2,1)}, f32[512,512]{1,0:T(8,128)}, bf16[1024,256]{1,0:T(8,128)(2,1)}, bf16[1024,256]{1,0:T(8,128)(2,1)}) custom-call(bf16[512,512]{1,0:T(8,128)(2,1)} %og_hbm.1, bf16[512,512]{1,0:T(8,128)(2,1)} %ig_ref.1, bf16[512,512]{1,0:T(8,128)(2,1)} %val_ref.1, bf16[512,512]{1,0:T(8,128)(2,1)} %fil_hbm.1, ...), custom_call_target="tpu_custom_call" | custom-call | tf_op jit(solution)/shard_map/pallas_call | solution.py:435
  92.8 0.0 copy-done.1
  92.8 0.0 copy-done
  92.8 0.0 copy-start.2
  92.8 1.2 %copy-done.2 = f32[512,512]{1,0:T(8,128)S(1)} copy-done((f32[512,512]{1,0:T(8,128)S(1)}, f32[512,512]{1,0:T(8,128)}, u32[]{:S(2)}) %copy-start.2) | copy-done | bytes 1048600
  94.0 0.0 copy-start.3
  94.0 1.0 %copy-done.3 = bf16[128,2048]{1,0:T(8,128)(2,1)S(1)} copy-done((bf16[128,2048]{1,0:T(8,128)(2,1)S(1)}, bf16[128,2048]{1,0:T(8,128)(2,1)}, u32[]{:S(2)}) %copy-start.3) | copy-done | bytes 524312
  95.1 0.0 copy-start.4
  95.1 1.0 %copy-done.4 = bf16[1024,256]{1,0:T(8,128)(2,1)S(1)} copy-done((bf16[1024,256]{1,0:T(8,128)(2,1)S(1)}, bf16[1024,256]{1,0:T(8,128)(2,1)}, u32[]{:S(2)}) %copy-start.4) | copy-done | bytes 524312
  96.1 0.0 copy-start.5
  96.1 1.0 %copy-done.5 = bf16[1024,256]{1,0:T(8,128)(2,1)S(1)} copy-done((bf16[1024,256]{1,0:T(8,128)(2,1)S(1)}, bf16[1024,256]{1,0:T(8,128)(2,1)}, u32[]{:S(2)}) %copy-start.5) | copy-done | bytes 524312
  97.2 2.9 %shard_map.156 = (f32[512,512]{1,0:T(8,128)}, f32[512,512]{1,0:T(8,128)}, f32[512,512]{1,0:T(8,128)}, f32[512,512]{1,0:T(8,128)}, bf16[128,2048]{1,0:T(8,128)(2,1)}) custom-call(bf16[512,512]{1,0:T(8,128)(2,1)S(1)} %copy-done, bf16[512,512]{1,0:T(8,128)(2,1)S(1)} %copy-done.1, bf16[1024,256]{1,0:T(8,128)(2,1)S(1)} %copy-done.4, ...), custom_call_target="tpu_custom_call" | custom-call | tf_op jit(solution)/shard_map/pallas_call | solution.py:473
Async XLA Ops:
  0.6 92.2 %copy-start.1 = (bf16[512,512]{1,0:T(8,128)(2,1)S(1)}, bf16[512,512]{1,0:T(8,128)(2,1)}, u32[]{:S(2)}) copy-start(bf16[512,512]{1,0:T(8,128)(2,1)} %val_ref.1) | copy-start | bytes 1572868
  0.6 92.2 %copy-start = (bf16[512,512]{1,0:T(8,128)(2,1)S(1)}, bf16[512,512]{1,0:T(8,128)(2,1)}, u32[]{:S(2)}) copy-start(bf16[512,512]{1,0:T(8,128)(2,1)} %ig_ref.1) | copy-start | bytes 1572868
  92.8 1.2 %copy-start.2 = (f32[512,512]{1,0:T(8,128)S(1)}, f32[512,512]{1,0:T(8,128)}, u32[]{:S(2)}) copy-start(f32[512,512]{1,0:T(8,128)} %get-tuple-element.16.d_og_in) | copy-start | bytes 3145732
  94.0 1.0 %copy-start.3 = (bf16[128,2048]{1,0:T(8,128)(2,1)S(1)}, bf16[128,2048]{1,0:T(8,128)(2,1)}, u32[]{:S(2)}) copy-start(bf16[128,2048]{1,0:T(8,128)(2,1)} %get-tuple-element.17.out_in) | copy-start | bytes 1572868
  95.1 1.0 %copy-start.4 = (bf16[1024,256]{1,0:T(8,128)(2,1)S(1)}, bf16[1024,256]{1,0:T(8,128)(2,1)}, u32[]{:S(2)}) copy-start(bf16[1024,256]{1,0:T(8,128)(2,1)} %get-tuple-element.14.ds_ref) | copy-start | bytes 1572868
  96.1 1.0 %copy-start.5 = (bf16[1024,256]{1,0:T(8,128)(2,1)S(1)}, bf16[1024,256]{1,0:T(8,128)(2,1)}, u32[]{:S(2)}) copy-start(bf16[1024,256]{1,0:T(8,128)(2,1)} %get-tuple-element.15.dk_ref) | copy-start | bytes 1572868

commit v3 on v2

--- a/solution.py
+++ b/solution.py
@@ -81,6 +81,16 @@
     my_tile, my_group = lax.rem(me, tiles), me // tiles
     my_slot = my_tile * groups + my_group
 
+    barrier = pltpu.get_barrier_semaphore()
+
+    def greet(d, _):
+        pl.semaphore_signal(barrier, inc=1, device_id=(lax.rem(me + d, parts), ch), device_id_type=MESH)
+        return 0
+
+    pl.semaphore_signal(barrier, inc=1, device_id=(me, core_peer), device_id_type=MESH)
+    pl.semaphore_signal(barrier, inc=1, device_id=(me, y_peer), device_id_type=MESH)
+    lax.fori_loop(1, parts, greet, 0)
+
     loads = {}
     for i, (name, src, dst) in enumerate(
         (
@@ -105,36 +115,30 @@
         for name in names:
             loads[name].wait()
 
-    barrier = pltpu.get_barrier_semaphore()
-
-    def greet(d, _):
-        pl.semaphore_signal(barrier, inc=1, device_id=(lax.rem(me + d, parts), ch), device_id_type=MESH)
-        return 0
-
-    pl.semaphore_signal(barrier, inc=1, device_id=(me, core_peer), device_id_type=MESH)
-    pl.semaphore_signal(barrier, inc=1, device_id=(me, y_peer), device_id_type=MESH)
-    lax.fori_loop(1, parts, greet, 0)
-
     def message(p):
         return pl.ds(pl.multiple_of(p * msg, msg), msg)
 
-    def send_one(slot, src_slot, dst, p):
-        pltpu.make_async_remote_copy(
-            src_ref=snd.at[slot, message(src_slot)],
-            dst_ref=dst,
-            send_sem=snd_sem.at[slot],
-            recv_sem=rcv_sem.at[slot],
-            device_id=(p, ch),
-            device_id_type=MESH,
-        ).start()
-
-    def send_back(slot, dst):
+    near_parts = parts // 2
+    side, place = me // near_parts, lax.rem(me, near_parts)
+
+    def send(slot, crossing, back=False, landing=None):
+        landing = rcv.at[slot] if landing is None else landing
+        base = (1 - side if crossing else side) * near_parts
+
         def go(i, _):
-            p = lax.rem(me + lax.rem(i * 37, parts), parts)
-            send_one(slot, p, dst, p)
-            return 0
-
-        lax.fori_loop(1, parts, go, 0)
+            p = base + lax.rem(place + lax.rem(i * 13, near_parts), near_parts)
+            by_channel = lax.rem(p, tiles) * groups + p // tiles
+            pltpu.make_async_remote_copy(
+                src_ref=snd.at[slot, message(p if back else by_channel)],
+                dst_ref=landing.at[message(my_slot if back else me)],
+                send_sem=snd_sem.at[slot],
+                recv_sem=rcv_sem.at[slot],
+                device_id=(p, ch),
+                device_id_type=MESH,
+            ).start()
+            return 0
+
+        lax.fori_loop(0 if crossing else 1, near_parts, go, 0)
 
     def await_bytes(ref, sem):
         ref = ref.at[pl.ds(0, (parts - 1) * msg)]
@@ -148,27 +152,15 @@
         both = jnp.concatenate([first.reshape(n, GROUP, half), second.reshape(n, GROUP, half)], 1)
         snd[slot, pl.ds(row, n * msg)] = both.reshape(n * msg, half).astype(BF16)
 
-    def send_tile(slot, load, u):
-        t = lax.rem(my_tile + u, tiles)
-        cols = pl.ds(pl.multiple_of(t * tile, tile), tile)
-        first, second = (load(pl.ds(h * half, half), cols).T for h in range(2))
-        to_messages(slot, first, second, pl.multiple_of(t * groups * msg, groups * msg))
-
-        def go(i, _):
-            j = lax.rem(my_group + i, groups)
-            send_one(slot, t * groups + j, rcv.at[slot, message(me)], j * tiles + t)
-            return 0
-
-        lax.fori_loop(jnp.maximum(1 - u, 0), groups, go, 0)
-
-    def send_tiles(slot, load, start, stop):
-        def go(u, _):
-            send_tile(slot, load, u)
-            return 0
-
-        lax.fori_loop(start, stop, go, 0)
-        if start == 0:
-            rcv[slot, message(me)] = snd[slot, message(my_slot)]
+    def pack(slot, load):
+        def go(t, _):
+            cols = pl.ds(pl.multiple_of(t * tile, tile), tile)
+            first, second = (load(pl.ds(h * half, half), cols).T for h in range(2))
+            to_messages(slot, first, second, pl.multiple_of(t * groups * msg, groups * msg))
+            return 0
+
+        lax.fori_loop(0, tiles, go, 0)
+        rcv[slot, message(me)] = snd[slot, message(my_slot)]
 
     def turn(real, imag, cols):
         a, b = turn_re_ref[:, cols], turn_im_ref[:, cols]
@@ -264,18 +256,22 @@
     cot_core = to_chan(2, cots.at[ch], cots.at[ch], core_peer, cot_snd_sem, cot_rcv_sem)
     cot_far = [cot_copy(3 + h, y_peer, h, core_peer) for h in range(2)]
 
-    loaded("cot", "fil")
+    loaded("fil")
+    pack(K_SLOT, lambda r, c: fil_ref[r, c].astype(F32))
+    loaded("cot")
     pl.semaphore_wait(barrier, parts + 1)
     cot_y[0].start()
     cot_y[1].start()
     cot_core.start()
-    send_tiles(K_SLOT, lambda r, c: fil_ref[r, c].astype(F32), 0, tiles)
+    send(K_SLOT, False)
     loaded("ig", "val")
 
     def source(r, c):
         return ig_ref[r, c].astype(F32) * val_ref[r, c].astype(F32)
 
-    send_tiles(S_SLOT, source, 0, tiles // 2)
+    pack(S_SLOT, source)
+    send(S_SLOT, False)
+    send(K_SLOT, True)
     loaded("w", "og")
 
     def d_block(b):
@@ -285,17 +281,19 @@
         time_buf[at] = d * og_ref[at].astype(F32)
 
     d_block(ch)
+    cot_core.wait_recv()
+    d_block(core_peer)
     for h in range(2):
         cot_y[h].wait_recv()
         cot_far[h].start()
-    send_tiles(S_SLOT, source, tiles // 2, tiles)
+    send(S_SLOT, True)
     d_block(y_peer)
-    cot_core.wait_recv()
-    d_block(core_peer)
     cot_far[0].wait_recv()
     cot_far[1].wait_recv()
     d_block(far_peer)
-    send_tiles(D_SLOT, lambda r, c: time_buf[r, c], 0, tiles)
+    pack(D_SLOT, lambda r, c: time_buf[r, c])
+    send(D_SLOT, False)
+    send(D_SLOT, True)
 
     loaded("across", "turn_re", "turn_im", "within_hi", "within_lo", "back")
     arrived(K_SLOT)
@@ -309,7 +307,8 @@
         return a * c - b * d, -(a * d + b * c)
 
     inverse(C_SLOT, conv_product)
-    send_back(C_SLOT, rcv.at[C_SLOT, message(my_slot)])
+    send(C_SLOT, False, back=True)
+    send(C_SLOT, True, back=True)
     rcv[C_SLOT, message(my_slot)] = snd[C_SLOT, message(me)]
     arrived(D_SLOT)
     forward(D_SLOT, 2)
@@ -323,7 +322,8 @@
         return product
 
     inverse(DS_SLOT, correlation(0))
-    send_back(DS_SLOT, ds_hbm.at[message(my_slot)])
+    send(DS_SLOT, True, back=True, landing=ds_hbm)
+    send(DS_SLOT, False, back=True, landing=ds_hbm)
     own_ds = pltpu.make_async_copy(snd.at[DS_SLOT, message(me)], ds_hbm.at[message(my_slot)], store_sem.at[0])
     own_ds.start()
     inverse(DK_SLOT, correlation(1))
@@ -332,20 +332,20 @@
 
     arrived(C_SLOT)
 
-    def use_conv(t, _):
-        cols = pl.ds(pl.multiple_of(t * tile, tile), tile)
-        both = rcv[C_SLOT, pl.ds(pl.multiple_of(t * groups * msg, groups * msg), groups * msg)]
-        both = both.astype(F32).reshape(groups, msg, half)
-        for h in range(2):
-            conv = both[:, h * GROUP : (h + 1) * GROUP].reshape(tile, half).T
-            at = pl.ds(h * half, half)
+    def use_conv(h):
+        at = pl.ds(pl.multiple_of(h * half, half), half)
+
+        def go(t, _):
+            cols = pl.ds(pl.multiple_of(t * tile, tile), tile)
+            both = rcv[C_SLOT, pl.ds(pl.multiple_of(t * groups * msg, groups * msg), groups * msg)]
+            both = both.astype(F32).reshape(groups, msg, half)
+            conv = jnp.where(h == 0, both[:, :GROUP], both[:, GROUP:]).reshape(tile, half).T
             gated[at, cols] = (og_ref[at, cols].astype(F32) * conv).astype(BF16)
             d_og_buf[at, cols] = d_gated[at, cols] * conv
-        return 0
-
-    lax.fori_loop(0, tiles, use_conv, 0)
-    d_og_out = pltpu.make_async_copy(d_og_buf, d_og_hbm, store_sem.at[2])
-    d_og_out.start()
+            return 0
+
+        lax.fori_loop(0, tiles, go, 0)
+
     out_tile = min(512, dout)
 
     def project(j, of_core, store):
@@ -372,15 +372,20 @@
 
     red_core = [to_chan(i, core_snd.at[i], core_rcv.at[i], core_peer, red_snd_sem, red_rcv_sem) for i in range(2)]
     red_y = to_chan(2, y_snd, y_rcv, y_peer, red_snd_sem, red_rcv_sem)
+    use_conv(1 - high)
     project(1 - high, 1 - core, store_peer(0))
     red_core[0].start()
     project(1 - high, core, store_mine(0))
     red_core[0].wait_recv()
     y_snd[...] = (total_buf[0] + core_rcv[0].astype(F32)).astype(BF16)
     red_y.start()
+    send(DK_SLOT, False, back=True, landing=dk_hbm)
+    send(DK_SLOT, True, back=True, landing=dk_hbm)
+    use_conv(high)
+    d_og_out = pltpu.make_async_copy(d_og_buf, d_og_hbm, store_sem.at[2])
+    d_og_out.start()
     project(high, 1 - core, store_peer(1))
     red_core[1].start()
-    send_back(DK_SLOT, dk_hbm.at[message(my_slot)])
     project(high, core, store_mine(1))
     red_core[1].wait_recv()
     total_buf[1] = total_buf[1] + core_rcv[1].astype(F32)
@@ -476,7 +481,7 @@
         out_shape=(grad, grad, grad, grad, block_out),
         in_specs=[by_channel, by_channel, by_row, by_row, by_channel, out_rows],
         out_specs=(by_channel, by_channel, by_channel, by_channel, out_rows),
-        compiler_params=pltpu.CompilerParams(vmem_limit_bytes=40 * 2**20),
+        compiler_params=pltpu.CompilerParams(vmem_limit_bytes=60 * 2**20),
     )(in_gate, values, ds_raw, dk_raw, d_og, output)
     return output, d_og, d_ig, d_val, d_fil
 

time: 100 us -> 93.9 us (0.939)
  local copies, waits for them, and re-layouts: 4.35 us -> 0 us
  Pallas kernels: 95 us -> 93.1 us
    unnamed x12 -> x0, local copies, waits for them, and re-layouts: 4.35 us -> none
    pallas_call x1, Pallas kernels: 92.1 us -> 88.3 us  [on_device(): pl.pallas_call(kernel, out_shape=(block_out, grad, raw, raw), in_specs=[a...]
    pallas_call x1, Pallas kernels: 2.87 us -> 4.83 us  [on_device(): pl.pallas_call(finish, grid=(tiles,), out_shape=(grad, grad, grad, grad,...]
where the time goes in v3:
time: 93.9 us; the launch traced here: 93.7 us
  Pallas kernels  93.1 us (99%)
    pallas_call x1, Pallas kernels, on_device(): pl.pallas_call(kernel, out_shape=(block_out, grad, raw, raw), in_specs=[a...  88.3 us
    pallas_call x1, Pallas kernels, on_device(): pl.pallas_call(finish, grid=(tiles,), out_shape=(grad, grad, grad, grad,...  4.83 us

profile of v3, /device:TPU:1, one launch (start us, length us, event | category | flops | bytes accessed | tf_op | source)
XLA Modules:
  0.0 93.7 jit_solution(2003402137756988429)
XLA Ops:
  0.6 88.3 %shard_map.155 = (bf16[128,2048]{1,0:T(8,128)(2,1)}, f32[512,512]{1,0:T(8,128)}, bf16[1024,256]{1,0:T(8,128)(2,1)}, bf16[1024,256]{1,0:T(8,128)(2,1)}) custom-call(bf16[512,512]{1,0:T(8,128)(2,1)} %og_hbm.1, bf16[512,512]{1,0:T(8,128)(2,1)} %ig_ref.1, bf16[512,512]{1,0:T(8,128)(2,1)} %val_ref.1, bf16[512,512]{1,0:T(8,128)(2,1)} %fil_hbm.1, ...), custom_call_target="tpu_custom_call" | custom-call | tf_op jit(solution)/shard_map/pallas_call | solution.py:440
  88.9 4.8 %shard_map.156 = (f32[512,512]{1,0:T(8,128)}, f32[512,512]{1,0:T(8,128)}, f32[512,512]{1,0:T(8,128)}, f32[512,512]{1,0:T(8,128)}, bf16[128,2048]{1,0:T(8,128)(2,1)}) custom-call(bf16[512,512]{1,0:T(8,128)(2,1)} %ig_ref.1, bf16[512,512]{1,0:T(8,128)(2,1)} %val_ref.1, bf16[1024,256]{1,0:T(8,128)(2,1)} %get-tuple-element.14.ds_ref, ...), custom_call_target="tpu_custom_call" | custom-call | tf_op jit(solution)/shard_map/pallas_call | solution.py:478

commit v4 on v3

--- a/solution.py
+++ b/solution.py
@@ -39,14 +39,14 @@
     factor = weight / (total * math.sqrt(total))
     back = np.concatenate([np.kron((np.cos(angle) * factor[:, None]).T, eye), np.kron((np.sin(angle) * factor[:, None]).T, eye)], 1)
     back_high, back_low = split_table(back)
-    back_table = np.concatenate([back_high, back_high, back_low], 1)
+    back_table = np.concatenate([back_high, back_low, back_high], 1)
     square = 2.0 * np.pi * ((pos[:, None] * pos[None, :]) % rows) / rows
     within = np.block([[np.cos(square), -np.sin(square)], [np.sin(square), np.cos(square)]])
-    within_high, within_low = split_table(within)
+    within_table = split_table(within)[0]
     turn = 2.0 * np.pi * (k1[:, None] * pos[None, :]) / total
     turn_re = np.repeat(np.cos(turn), GROUP, 0).astype(np.float32)
     turn_im = np.repeat(-np.sin(turn), GROUP, 0).astype(np.float32)
-    return across_table, within_high, within_low, back_table, turn_re, turn_im
+    return across_table, within_table, back_table, turn_re, turn_im
 
 
 def split_value(value):
@@ -54,12 +54,24 @@
     return high, (value - high.astype(F32)).astype(BF16)
 
 
+def by_fours(start, stop, do):
+    for i in range(start, 4 if start else 0):
+        do(i)
+
+    def go(n, _):
+        for i in range(4):
+            do(n * 4 + i)
+        return 0
+
+    lax.fori_loop(1 if start else 0, stop // 4, go, 0)
+
+
 def kernel(
     og_hbm, ig_hbm, val_hbm, fil_hbm, w_hbm, cot_hbm,
-    across_hbm, within_hi_hbm, within_lo_hbm, back_hbm, turn_re_hbm, turn_im_hbm,
+    across_hbm, within_hbm, back_hbm, turn_re_hbm, turn_im_hbm,
     out_hbm, d_og_hbm, ds_hbm, dk_hbm,
     og_ref, ig_ref, val_ref, fil_ref, w_ref,
-    across_ref, within_hi_ref, within_lo_ref, back_ref, turn_re_ref, turn_im_ref,
+    across_ref, within_ref, back_ref, turn_re_ref, turn_im_ref,
     snd, rcv, cots, d_gated, time_buf, gated, d_og_buf, chan_buf, lhs, spec, stack,
     core_snd, core_rcv, y_snd, y_rcv, total_buf, out_buf,
     load_sem, store_sem, snd_sem, rcv_sem, cot_snd_sem, cot_rcv_sem, red_snd_sem, red_rcv_sem,
@@ -81,16 +93,6 @@
     my_tile, my_group = lax.rem(me, tiles), me // tiles
     my_slot = my_tile * groups + my_group
 
-    barrier = pltpu.get_barrier_semaphore()
-
-    def greet(d, _):
-        pl.semaphore_signal(barrier, inc=1, device_id=(lax.rem(me + d, parts), ch), device_id_type=MESH)
-        return 0
-
-    pl.semaphore_signal(barrier, inc=1, device_id=(me, core_peer), device_id_type=MESH)
-    pl.semaphore_signal(barrier, inc=1, device_id=(me, y_peer), device_id_type=MESH)
-    lax.fori_loop(1, parts, greet, 0)
-
     loads = {}
     for i, (name, src, dst) in enumerate(
         (
@@ -103,18 +105,32 @@
             ("across", across_hbm, across_ref),
             ("turn_re", turn_re_hbm, turn_re_ref),
             ("turn_im", turn_im_hbm, turn_im_ref),
-            ("within_hi", within_hi_hbm, within_hi_ref),
-            ("within_lo", within_lo_hbm, within_lo_ref),
+            ("within", within_hbm, within_ref),
             ("back", back_hbm, back_ref),
         )
     ):
         loads[name] = pltpu.make_async_copy(src, dst, load_sem.at[i])
-        loads[name].start()
 
     def loaded(*names):
         for name in names:
             loads[name].wait()
 
+    loads["fil"].start()
+    loads["cot"].start()
+
+    barrier = pltpu.get_barrier_semaphore()
+
+    def greet(d):
+        pl.semaphore_signal(barrier, inc=1, device_id=(lax.rem(me + d, parts), ch), device_id_type=MESH)
+
+    by_fours(1, parts, greet)
+    pl.semaphore_signal(barrier, inc=1, device_id=(me, core_peer), device_id_type=MESH)
+    pl.semaphore_signal(barrier, inc=1, device_id=(me, y_peer), device_id_type=MESH)
+
+    for name, load in loads.items():
+        if name not in ("fil", "cot"):
+            load.start()
+
     def message(p):
         return pl.ds(pl.multiple_of(p * msg, msg), msg)
 
@@ -125,8 +141,8 @@
         landing = rcv.at[slot] if landing is None else landing
         base = (1 - side if crossing else side) * near_parts
 
-        def go(i, _):
-            p = base + lax.rem(place + lax.rem(i * 13, near_parts), near_parts)
+        def start(i):
+            p = base + lax.rem(place + i * 13, near_parts)
             by_channel = lax.rem(p, tiles) * groups + p // tiles
             pltpu.make_async_remote_copy(
                 src_ref=snd.at[slot, message(p if back else by_channel)],
@@ -136,9 +152,8 @@
                 device_id=(p, ch),
                 device_id_type=MESH,
             ).start()
-            return 0
-
-        lax.fori_loop(0 if crossing else 1, near_parts, go, 0)
+
+        by_fours(0 if crossing else 1, near_parts, start)
 
     def await_bytes(ref, sem):
         ref = ref.at[pl.ds(0, (parts - 1) * msg)]
@@ -166,11 +181,14 @@
         a, b = turn_re_ref[:, cols], turn_im_ref[:, cols]
         return real * a - imag * b, real * b + imag * a
 
-    def put_lhs(real, imag, cols, cols_imag):
+    def put_lhs(real, imag, cols, cols_imag, fine):
         for value, at in ((real, cols), (imag, cols_imag)):
-            hi, lo = split_value(value)
-            lhs[:nk, at] = hi
-            lhs[nk:, at] = lo
+            if fine:
+                hi, lo = split_value(value)
+                lhs[:nk, at] = hi
+                lhs[nk:, at] = lo
+            else:
+                lhs[:nk, at] = value.astype(BF16)
 
     def halves_of(h):
         return (
@@ -178,19 +196,21 @@
             pl.ds(pl.multiple_of(rows + h * half, half), half),
         )
 
-    def within(dst):
+    def within(dst, fine):
         def go(j, _):
             cols = pl.ds(pl.multiple_of(j * half, half), half)
-            both = jnp.dot(lhs[...], within_hi_ref[:, cols], preferred_element_type=F32)
-            rest = jnp.dot(lhs[:nk], within_lo_ref[:, cols], preferred_element_type=F32)
-            spec[dst, :, cols] = both[:nk] + both[nk:] + rest
+            if fine:
+                both = jnp.dot(lhs[...], within_ref[:, cols], preferred_element_type=F32)
+                spec[dst, :, cols] = both[:nk] + both[nk:]
+            else:
+                spec[dst, :, cols] = jnp.dot(lhs[:nk], within_ref[:, cols], preferred_element_type=F32)
             return 0
 
         lax.fori_loop(0, 4, go, 0)
 
     step = min(16, parts)
 
-    def forward(slot, dst):
+    def forward(slot, dst, fine):
         def regroup(i, _):
             both = rcv[slot, pl.ds(pl.multiple_of(i * step * msg, step * msg), step * msg)]
             both = both.astype(F32).reshape(step, msg, half)
@@ -203,24 +223,27 @@
 
         def go(h, _):
             cols, cols_imag = halves_of(h)
-            y = jnp.dot(across_ref[...], chan_buf[:, cols], preferred_element_type=F32)
-            y = y[: 2 * nk] + y[2 * nk :]
+            if fine:
+                y = jnp.dot(across_ref[...], chan_buf[:, cols], preferred_element_type=F32)
+                y = y[: 2 * nk] + y[2 * nk :]
+            else:
+                y = jnp.dot(across_ref[: 2 * nk], chan_buf[:, cols], preferred_element_type=F32)
             real, imag = turn(y[:nk], y[nk:], cols)
-            put_lhs(real, imag, cols, cols_imag)
+            put_lhs(real, imag, cols, cols_imag, True)
             return 0
 
         lax.fori_loop(0, 2, go, 0)
-        within(dst)
-
-    def inverse(slot, product):
+        within(dst, True)
+
+    def inverse(slot, product, fine):
         def fill(h, _):
             cols, cols_imag = halves_of(h)
             real, imag = product(cols, cols_imag)
-            put_lhs(real, imag, cols, cols_imag)
+            put_lhs(real, imag, cols, cols_imag, fine)
             return 0
 
         lax.fori_loop(0, 2, fill, 0)
-        within(3)
+        within(3, fine)
 
         def go(h, _):
             cols, cols_imag = halves_of(h)
@@ -228,9 +251,15 @@
             for i, value in enumerate((real, imag)):
                 hi, lo = split_value(value)
                 stack[i * nk : (i + 1) * nk, cols] = hi
-                stack[(2 + i) * nk : (3 + i) * nk, cols] = lo
-                stack[(4 + i) * nk : (5 + i) * nk, cols] = hi
-            time_buf[:, cols] = jnp.dot(back_ref[...], stack[:, cols], preferred_element_type=F32)
+                stack[(2 + i) * nk : (3 + i) * nk, cols] = hi
+                if fine:
+                    stack[(4 + i) * nk : (5 + i) * nk, cols] = lo
+            if fine:
+                time_buf[:, cols] = jnp.dot(back_ref[...], stack[:, cols], preferred_element_type=F32)
+            else:
+                time_buf[:, cols] = jnp.dot(
+                    back_ref[:, : 4 * nk], stack[: 4 * nk, cols], preferred_element_type=F32
+                )
             return 0
 
         lax.fori_loop(0, 2, go, 0)
@@ -293,25 +322,25 @@
     d_block(far_peer)
     pack(D_SLOT, lambda r, c: time_buf[r, c])
     send(D_SLOT, False)
+
+    loaded("across", "turn_re", "turn_im", "within", "back")
+    arrived(K_SLOT)
+    forward(K_SLOT, 0, True)
     send(D_SLOT, True)
-
-    loaded("across", "turn_re", "turn_im", "within_hi", "within_lo", "back")
-    arrived(K_SLOT)
-    forward(K_SLOT, 0)
     arrived(S_SLOT)
-    forward(S_SLOT, 1)
+    forward(S_SLOT, 1, True)
 
     def conv_product(cols, cols_imag):
         a, b = spec[0, :, cols], spec[0, :, cols_imag]
         c, d = spec[1, :, cols], spec[1, :, cols_imag]
         return a * c - b * d, -(a * d + b * c)
 
-    inverse(C_SLOT, conv_product)
+    inverse(C_SLOT, conv_product, True)
     send(C_SLOT, False, back=True)
     send(C_SLOT, True, back=True)
     rcv[C_SLOT, message(my_slot)] = snd[C_SLOT, message(me)]
     arrived(D_SLOT)
-    forward(D_SLOT, 2)
+    forward(D_SLOT, 2, False)
 
     def correlation(which):
         def product(cols, cols_imag):
@@ -321,14 +350,11 @@
 
         return product
 
-    inverse(DS_SLOT, correlation(0))
+    inverse(DS_SLOT, correlation(0), False)
     send(DS_SLOT, True, back=True, landing=ds_hbm)
     send(DS_SLOT, False, back=True, landing=ds_hbm)
     own_ds = pltpu.make_async_copy(snd.at[DS_SLOT, message(me)], ds_hbm.at[message(my_slot)], store_sem.at[0])
     own_ds.start()
-    inverse(DK_SLOT, correlation(1))
-    own_dk = pltpu.make_async_copy(snd.at[DK_SLOT, message(me)], dk_hbm.at[message(my_slot)], store_sem.at[1])
-    own_dk.start()
 
     arrived(C_SLOT)
 
@@ -379,6 +405,9 @@
     red_core[0].wait_recv()
     y_snd[...] = (total_buf[0] + core_rcv[0].astype(F32)).astype(BF16)
     red_y.start()
+    inverse(DK_SLOT, correlation(1), False)
+    own_dk = pltpu.make_async_copy(snd.at[DK_SLOT, message(me)], dk_hbm.at[message(my_slot)], store_sem.at[1])
+    own_dk.start()
     send(DK_SLOT, False, back=True, landing=dk_hbm)
     send(DK_SLOT, True, back=True, landing=dk_hbm)
     use_conv(high)
@@ -428,7 +457,7 @@
     parts = lax.axis_size("seq")
     blk, dout = out_cotangent.shape
     tables = make_tables(parts, rows)
-    nk = tables[4].shape[0]
+    nk = tables[3].shape[0]
     msgs = (parts * 2 * GROUP, rows // 2)
     tile = min(TILE, width)
     tiles = width // tile
@@ -440,7 +469,7 @@
     output, d_og, ds_raw, dk_raw = pl.pallas_call(
         kernel,
         out_shape=(block_out, grad, raw, raw),
-        in_specs=[anywhere] * 12,
+        in_specs=[anywhere] * 11,
         out_specs=(anywhere,) * 4,
         scratch_shapes=[
             *(pltpu.VMEM(x.shape, x.dtype) for i, x in enumerate(operands) if i != 5),
@@ -461,7 +490,7 @@
             pltpu.VMEM((blk, dout), BF16),
             pltpu.VMEM((2, blk, dout), F32),
             pltpu.VMEM((blk, dout), BF16),
-            pltpu.SemaphoreType.DMA((12,)),
+            pltpu.SemaphoreType.DMA((11,)),
             pltpu.SemaphoreType.DMA((4,)),
             pltpu.SemaphoreType.DMA((6,)),
             pltpu.SemaphoreType.DMA((6,)),

time: 93.9 us -> 92.3 us (0.983)
  Pallas kernels: 93.1 us -> 91.5 us
    pallas_call x1, Pallas kernels: 88.3 us -> 86.6 us  [on_device(): pl.pallas_call(kernel, out_shape=(block_out, grad, raw, raw), in_specs=[a...]
where the time goes in v4:
time: 92.3 us; the launch traced here: 92.1 us
  Pallas kernels  91.5 us (99%)
    pallas_call x1, Pallas kernels, on_device(): pl.pallas_call(kernel, out_shape=(block_out, grad, raw, raw), in_specs=[a...  86.6 us
    pallas_call x1, Pallas kernels, on_device(): pl.pallas_call(finish, grid=(tiles,), out_shape=(grad, grad, grad, grad,...  4.83 us

profile of v4, /device:TPU:1, one launch (start us, length us, event | category | flops | bytes accessed | tf_op | source)
XLA Modules:
  0.0 92.1 jit_solution(11407920722273662928)
XLA Ops:
  0.6 86.6 %shard_map.146 = (bf16[128,2048]{1,0:T(8,128)(2,1)}, f32[512,512]{1,0:T(8,128)}, bf16[1024,256]{1,0:T(8,128)(2,1)}, bf16[1024,256]{1,0:T(8,128)(2,1)}) custom-call(bf16[512,512]{1,0:T(8,128)(2,1)} %og_hbm.1, bf16[512,512]{1,0:T(8,128)(2,1)} %ig_ref.1, bf16[512,512]{1,0:T(8,128)(2,1)} %val_ref.1, bf16[512,512]{1,0:T(8,128)(2,1)} %fil_hbm.1, ...), custom_call_target="tpu_custom_call" | custom-call | tf_op jit(solution)/shard_map/pallas_call | solution.py:469
  87.3 4.8 %shard_map.147 = (f32[512,512]{1,0:T(8,128)}, f32[512,512]{1,0:T(8,128)}, f32[512,512]{1,0:T(8,128)}, f32[512,512]{1,0:T(8,128)}, bf16[128,2048]{1,0:T(8,128)(2,1)}) custom-call(bf16[512,512]{1,0:T(8,128)(2,1)} %ig_ref.1, bf16[512,512]{1,0:T(8,128)(2,1)} %val_ref.1, bf16[1024,256]{1,0:T(8,128)(2,1)} %get-tuple-element.14.ds_ref, ...), custom_call_target="tpu_custom_call" | custom-call | tf_op jit(solution)/shard_map/pallas_call | solution.py:507

commit v5 on v4

--- a/solution.py
+++ b/solution.py
@@ -72,7 +72,7 @@
     out_hbm, d_og_hbm, ds_hbm, dk_hbm,
     og_ref, ig_ref, val_ref, fil_ref, w_ref,
     across_ref, within_ref, back_ref, turn_re_ref, turn_im_ref,
-    snd, rcv, cots, d_gated, time_buf, gated, d_og_buf, chan_buf, lhs, spec, stack,
+    snd, rcv, cots, d_gated, time_buf, gated, d_og_buf, ds_buf, chan_buf, lhs, spec, stack,
     core_snd, core_rcv, y_snd, y_rcv, total_buf, out_buf,
     load_sem, store_sem, snd_sem, rcv_sem, cot_snd_sem, cot_rcv_sem, red_snd_sem, red_rcv_sem,
 ):
@@ -351,26 +351,30 @@
         return product
 
     inverse(DS_SLOT, correlation(0), False)
-    send(DS_SLOT, True, back=True, landing=ds_hbm)
-    send(DS_SLOT, False, back=True, landing=ds_hbm)
-    own_ds = pltpu.make_async_copy(snd.at[DS_SLOT, message(me)], ds_hbm.at[message(my_slot)], store_sem.at[0])
-    own_ds.start()
+    send(DS_SLOT, True, back=True)
+    send(DS_SLOT, False, back=True)
+    rcv[DS_SLOT, message(my_slot)] = snd[DS_SLOT, message(me)]
 
     arrived(C_SLOT)
 
-    def use_conv(h):
+    def unpack_half(slot, h, store):
         at = pl.ds(pl.multiple_of(h * half, half), half)
 
         def go(t, _):
             cols = pl.ds(pl.multiple_of(t * tile, tile), tile)
-            both = rcv[C_SLOT, pl.ds(pl.multiple_of(t * groups * msg, groups * msg), groups * msg)]
+            both = rcv[slot, pl.ds(pl.multiple_of(t * groups * msg, groups * msg), groups * msg)]
             both = both.astype(F32).reshape(groups, msg, half)
-            conv = jnp.where(h == 0, both[:, :GROUP], both[:, GROUP:]).reshape(tile, half).T
+            store(at, cols, jnp.where(h == 0, both[:, :GROUP], both[:, GROUP:]).reshape(tile, half).T)
+            return 0
+
+        lax.fori_loop(0, tiles, go, 0)
+
+    def use_conv(h):
+        def store(at, cols, conv):
             gated[at, cols] = (og_ref[at, cols].astype(F32) * conv).astype(BF16)
-            d_og_buf[at, cols] = d_gated[at, cols] * conv
-            return 0
-
-        lax.fori_loop(0, tiles, go, 0)
+            d_og_buf[at, cols] = (d_gated[at, cols] * conv).astype(BF16)
+
+        unpack_half(C_SLOT, h, store)
 
     out_tile = min(512, dout)
 
@@ -423,33 +427,68 @@
     out_out = pltpu.make_async_copy(out_buf, out_hbm, store_sem.at[3])
     out_out.start()
 
-    await_bytes(ds_hbm, rcv_sem.at[DS_SLOT])
+    def use_source(at, cols, grad):
+        ds_buf[at, cols] = grad.astype(BF16)
+
+    arrived(DS_SLOT)
+    for h in range(2):
+        unpack_half(DS_SLOT, h, use_source)
+    ds_out = pltpu.make_async_copy(ds_buf, ds_hbm, store_sem.at[0])
+    ds_out.start()
     for slot in range(6):
         await_bytes(snd.at[slot], snd_sem.at[slot])
     for copy in (*cot_y, cot_core, *cot_far, *red_core, red_y):
         copy.wait_send()
-    for copy in (own_ds, own_dk, d_og_out, out_out):
+    for copy in (ds_out, own_dk, d_og_out, out_out):
         copy.wait()
     await_bytes(dk_hbm, rcv_sem.at[DK_SLOT])
 
 
-def finish(ig_ref, val_ref, ds_ref, dk_ref, d_og_in, out_in, d_ig_ref, d_val_ref, d_fil_ref, d_og_ref, out_ref):
-    rows, tile = val_ref.shape
+def finish(
+    ig_hbm, val_hbm, ds_hbm, dk_hbm, d_og_in_hbm, out_in_hbm,
+    d_ig_hbm, d_val_hbm, d_fil_hbm, d_og_hbm, out_hbm,
+    ig, val, ds, dk, d_og_in, d_ig, d_val, d_fil, d_og, load_sem, store_sem,
+):
+    rows, width = ig.shape
     half = rows // 2
-    groups = tile // GROUP
-
-    def positions(ref, h):
-        both = ref[...].astype(F32).reshape(groups, 2 * GROUP, half)
-        return both[:, h * GROUP : (h + 1) * GROUP].reshape(tile, half).T
-
-    for h in range(2):
-        at = pl.ds(h * half, half)
-        grad = positions(ds_ref, h)
-        d_ig_ref[at] = grad * val_ref[at].astype(F32)
-        d_val_ref[at] = grad * ig_ref[at].astype(F32)
-        d_fil_ref[at] = positions(dk_ref, h)
-    d_og_ref[...] = d_og_in[...]
-    out_ref[...] = out_in[...]
+    loads, stores = [], []
+
+    def load(src, dst):
+        loads.append(pltpu.make_async_copy(src, dst, load_sem.at[len(loads)]))
+        loads[-1].start()
+
+    def store(src, dst):
+        stores.append(pltpu.make_async_copy(src, dst, store_sem.at[len(stores)]))
+        stores[-1].start()
+
+    halves = [pl.ds(h * half, half) for h in range(2)]
+    for at in halves:
+        for src, dst in ((ds_hbm, ds), (val_hbm, val), (ig_hbm, ig)):
+            load(src.at[at], dst.at[at])
+    load(dk_hbm, dk)
+    load(d_og_in_hbm, d_og_in)
+    store(out_in_hbm, out_hbm)
+    for h, at in enumerate(halves):
+        for copy in loads[3 * h : 3 * h + 3]:
+            copy.wait()
+        grad = ds[at].astype(F32)
+        d_ig[at] = grad * val[at].astype(F32)
+        store(d_ig.at[at], d_ig_hbm.at[at])
+        d_val[at] = grad * ig[at].astype(F32)
+        store(d_val.at[at], d_val_hbm.at[at])
+    tile = min(TILE, width)
+    msgs = 2 * tile
+    loads[6].wait()
+    for h, at in enumerate(halves):
+        for t in range(width // tile):
+            both = dk[pl.ds(t * msgs, msgs)].astype(F32).reshape(tile // GROUP, 2 * GROUP, half)
+            d_fil[at, pl.ds(t * tile, tile)] = both[:, h * GROUP : (h + 1) * GROUP].reshape(tile, half).T
+        store(d_fil.at[at], d_fil_hbm.at[at])
+    loads[7].wait()
+    d_og[...] = d_og_in[...].astype(F32)
+    store(d_og, d_og_hbm)
+    for copy in stores:
+        copy.wait()
 
 
 def on_device(out_gate, in_gate, values, filter_param, out_weight, out_cotangent):
@@ -459,27 +498,27 @@
     tables = make_tables(parts, rows)
     nk = tables[3].shape[0]
     msgs = (parts * 2 * GROUP, rows // 2)
-    tile = min(TILE, width)
-    tiles = width // tile
     operands = (out_gate, in_gate, values, filter_param, out_weight, out_cotangent, *tables)
     grad = jax.ShapeDtypeStruct((rows, width), F32)
     block_out = jax.ShapeDtypeStruct((blk, dout), BF16)
     raw = jax.ShapeDtypeStruct(msgs, BF16)
+    short = jax.ShapeDtypeStruct((rows, width), BF16)
     anywhere = pl.BlockSpec(memory_space=pl.ANY)
     output, d_og, ds_raw, dk_raw = pl.pallas_call(
         kernel,
-        out_shape=(block_out, grad, raw, raw),
+        out_shape=(block_out, short, short, raw),
         in_specs=[anywhere] * 11,
         out_specs=(anywhere,) * 4,
         scratch_shapes=[
             *(pltpu.VMEM(x.shape, x.dtype) for i, x in enumerate(operands) if i != 5),
             pltpu.VMEM((6, *msgs), BF16),
-            pltpu.VMEM((4, *msgs), BF16),
+            pltpu.VMEM((5, *msgs), BF16),
             pltpu.VMEM((4, blk, dout), BF16),
             pltpu.VMEM((rows, width), F32),
             pltpu.VMEM((rows, width), F32),
             pltpu.VMEM((rows, width), BF16),
-            pltpu.VMEM((rows, width), F32),
+            pltpu.VMEM((rows, width), BF16),
+            pltpu.VMEM((rows, width), BF16),
             pltpu.VMEM((parts * GROUP, rows), BF16),
             pltpu.VMEM((2 * nk, 2 * rows), BF16),
             pltpu.VMEM((4, nk, 2 * rows), F32),
@@ -501,15 +540,19 @@
         ],
         compiler_params=pltpu.CompilerParams(collective_id=0, has_side_effects=True, vmem_limit_bytes=60 * 2**20),
     )(*operands)
-    by_channel = pl.BlockSpec((rows, tile), lambda t: (0, t))
-    by_row = pl.BlockSpec((msgs[0] // tiles, msgs[1]), lambda t: (t, 0))
-    out_rows = pl.BlockSpec((blk // tiles, dout), lambda t: (t, 0))
     d_ig, d_val, d_fil, d_og, output = pl.pallas_call(
         finish,
-        grid=(tiles,),
         out_shape=(grad, grad, grad, grad, block_out),
-        in_specs=[by_channel, by_channel, by_row, by_row, by_channel, out_rows],
-        out_specs=(by_channel, by_channel, by_channel, by_channel, out_rows),
+        in_specs=[anywhere] * 6,
+        out_specs=(anywhere,) * 5,
+        scratch_shapes=[
+            *([pltpu.VMEM((rows, width), BF16)] * 3),
+            pltpu.VMEM(msgs, BF16),
+            pltpu.VMEM((rows, width), BF16),
+            *([pltpu.VMEM((rows, width), F32)] * 4),
+            pltpu.SemaphoreType.DMA((8,)),
+            pltpu.SemaphoreType.DMA((8,)),
+        ],
         compiler_params=pltpu.CompilerParams(vmem_limit_bytes=60 * 2**20),
     )(in_gate, values, ds_raw, dk_raw, d_og, output)
     return output, d_og, d_ig, d_val, d_fil

time: 92.3 us -> 105 us (1.14)
  Pallas kernels: 91.5 us -> 105 us
    pallas_call x2, Pallas kernels: 91.5 us -> 105 us  [the longest x1 87.5 us: on_device(): pl.pallas_call(kernel, out_shape=(block_out, short, short, raw), in_specs...]
where the time goes in v5:
time: 105 us
  Pallas kernels  105 us (100%)
    pallas_call x1, Pallas kernels, on_device(): pl.pallas_call(kernel, out_shape=(block_out, short, short, raw), in_specs...  87.5 us
    pallas_call x1, Pallas kernels, on_device(): pl.pallas_call(finish, out_shape=(grad, grad, grad, grad, block_out), in_...  17.1 us

profile of v5, /device:TPU:1, one launch (start us, length us, event | category | flops | bytes accessed | tf_op | source)
XLA Modules:
  0.0 105.3 jit_solution(17873919763935053350)
XLA Ops:
  0.6 87.5 %shard_map.146 = (bf16[128,2048]{1,0:T(8,128)(2,1)}, bf16[512,512]{1,0:T(8,128)(2,1)}, bf16[512,512]{1,0:T(8,128)(2,1)}, bf16[1024,256]{1,0:T(8,128)(2,1)}) custom-call(bf16[512,512]{1,0:T(8,128)(2,1)} %og_hbm.1, bf16[512,512]{1,0:T(8,128)(2,1)} %ig_hbm.3, bf16[512,512]{1,0:T(8,128)(2,1)} %val_hbm.3, bf16[512,512]{1,0:T(8,128)(2,1)} %fil_hbm.1, ...), custom_call_target="tpu_custom_call" | custom-call | tf_op jit(solution)/shard_map/pallas_call | solution.py:507
  88.1 17.1 %shard_map.147 = (f32[512,512]{1,0:T(8,128)}, f32[512,512]{1,0:T(8,128)}, f32[512,512]{1,0:T(8,128)}, f32[512,512]{1,0:T(8,128)}, bf16[128,2048]{1,0:T(8,128)(2,1)}) custom-call(bf16[512,512]{1,0:T(8,128)(2,1)} %ig_hbm.3, bf16[512,512]{1,0:T(8,128)(2,1)} %val_hbm.3, bf16[512,512]{1,0:T(8,128)(2,1)} %get-tuple-element.14.ds_hbm, ...), custom_call_target="tpu_custom_call" | custom-call | tf_op jit(solution)/shard_map/pallas_call | solution.py:543

commit v6 on v5

--- a/solution.py
+++ b/solution.py
@@ -447,7 +447,7 @@
 def finish(
     ig_hbm, val_hbm, ds_hbm, dk_hbm, d_og_in_hbm, out_in_hbm,
     d_ig_hbm, d_val_hbm, d_fil_hbm, d_og_hbm, out_hbm,
-    ig, val, ds, dk, d_og_in, d_ig, d_val, d_fil, d_og, load_sem, store_sem,
+    ig, val, ds, dk, d_og_in, out, d_ig, d_val, d_fil, d_og, load_sem, store_sem,
 ):
     rows, width = ig.shape
     half = rows // 2
@@ -467,7 +467,7 @@
             load(src.at[at], dst.at[at])
     load(dk_hbm, dk)
     load(d_og_in_hbm, d_og_in)
-    store(out_in_hbm, out_hbm)
+    load(out_in_hbm, out)
     for h, at in enumerate(halves):
         for copy in loads[3 * h : 3 * h + 3]:
             copy.wait()
@@ -484,6 +484,8 @@
             both = dk[pl.ds(t * msgs, msgs)].astype(F32).reshape(tile // GROUP, 2 * GROUP, half)
             d_fil[at, pl.ds(t * tile, tile)] = both[:, h * GROUP : (h + 1) * GROUP].reshape(tile, half).T
         store(d_fil.at[at], d_fil_hbm.at[at])
+    loads[8].wait()
+    store(out, out_hbm)
     loads[7].wait()
     d_og[...] = d_og_in[...].astype(F32)
     store(d_og, d_og_hbm)
@@ -549,8 +551,9 @@
             *([pltpu.VMEM((rows, width), BF16)] * 3),
             pltpu.VMEM(msgs, BF16),
             pltpu.VMEM((rows, width), BF16),
+            pltpu.VMEM((blk, dout), BF16),
             *([pltpu.VMEM((rows, width), F32)] * 4),
-            pltpu.SemaphoreType.DMA((8,)),
+            pltpu.SemaphoreType.DMA((9,)),
             pltpu.SemaphoreType.DMA((8,)),
         ],
         compiler_params=pltpu.CompilerParams(vmem_limit_bytes=60 * 2**20),

time: 105 us -> 91.7 us (0.87)
  Pallas kernels: 105 us -> 91 us
    pallas_call x1, Pallas kernels: 17.1 us -> 3.5 us  [on_device(): pl.pallas_call(finish, out_shape=(grad, grad, grad, grad, block_out), in_...]
where the time goes in v6:
time: 91.7 us; the launch traced here: 91.6 us
  Pallas kernels  91 us (99%)
    pallas_call x1, Pallas kernels, on_device(): pl.pallas_call(kernel, out_shape=(block_out, short, short, raw), in_specs...  87.5 us
    pallas_call x1, Pallas kernels, on_device(): pl.pallas_call(finish, out_shape=(grad, grad, grad, grad, block_out), in_...  3.5 us

profile of v6, /device:TPU:1, one launch (start us, length us, event | category | flops | bytes accessed | tf_op | source)
XLA Modules:
  0.0 91.6 jit_solution(10611735208090773550)
XLA Ops:
  0.6 87.5 %shard_map.146 = (bf16[128,2048]{1,0:T(8,128)(2,1)}, bf16[512,512]{1,0:T(8,128)(2,1)}, bf16[512,512]{1,0:T(8,128)(2,1)}, bf16[1024,256]{1,0:T(8,128)(2,1)}) custom-call(bf16[512,512]{1,0:T(8,128)(2,1)} %og_hbm.1, bf16[512,512]{1,0:T(8,128)(2,1)} %ig_hbm.3, bf16[512,512]{1,0:T(8,128)(2,1)} %val_hbm.3, bf16[512,512]{1,0:T(8,128)(2,1)} %fil_hbm.1, ...), custom_call_target="tpu_custom_call" | custom-call | tf_op jit(solution)/shard_map/pallas_call | solution.py:509
  88.1 3.5 %shard_map.147 = (f32[512,512]{1,0:T(8,128)}, f32[512,512]{1,0:T(8,128)}, f32[512,512]{1,0:T(8,128)}, f32[512,512]{1,0:T(8,128)}, bf16[128,2048]{1,0:T(8,128)(2,1)}) custom-call(bf16[512,512]{1,0:T(8,128)(2,1)} %ig_hbm.3, bf16[512,512]{1,0:T(8,128)(2,1)} %val_hbm.3, bf16[512,512]{1,0:T(8,128)(2,1)} %get-tuple-element.14.ds_hbm, ...), custom_call_target="tpu_custom_call" | custom-call | tf_op jit(solution)/shard_map/pallas_call | solution.py:545
